TPU v7x, 32 devices: a whole 2x2x4 slice. The times are simulated.
32 devices in a mesh: dp: 8 (over z, x), slot: 4 (over y, core).
Axes of the slice: x: 2, y: 2, z: 4, core: 2. Of those that a mesh axis runs over, the one named last changes fastest.
Arguments:
- inputs: float32 [16, 1024, 512], P('dp'), may hold values from -6 to 6
- starts: int32 [16, 1024], P('dp'), may hold values 0 or 1
- w_query: bfloat16 [512, 512], P(('dp', 'slot')), may hold values from -0.09375 to 0.09375
- w_key: bfloat16 [512, 512], P(('dp', 'slot')), may hold values from -0.25 to 0.25
- w_value: bfloat16 [512, 512], P(('dp', 'slot')), may hold values from -0.25 to 0.25
- w_out: bfloat16 [512, 512], P(('dp', 'slot')), may hold values from -1 to 1
- w_slot: bfloat16 [512, 512], P('dp', 'slot'), may hold values from -0.25 to 0.25
- w_up: bfloat16 [512, 2048], P('dp', 'slot'), may hold values from -0.25 to 0.25
- w_down: bfloat16 [2048, 512], P('slot', 'dp'), may hold values from -0.125 to 0.125
- gain_attn: bfloat16 [512], P(('dp', 'slot')), may hold values from 0.5 to 1.5
- gain_ffn: bfloat16 [512], P(('dp', 'slot')), may hold values from 0.5 to 1.5
- cotangent: float32 [16, 1024, 512], P('dp'), may hold values from -6 to 6
Outputs:
- output: float32 [16, 1024, 512], P('dp')
- grad_inputs: float32 [16, 1024, 512], P('dp')
- grad_query: float32 [512, 512], P(('dp', 'slot'))
- grad_key: float32 [512, 512], P(('dp', 'slot'))
- grad_value: float32 [512, 512], P(('dp', 'slot'))
- grad_out: float32 [512, 512], P(('dp', 'slot'))
- grad_slot: float32 [512, 512], P('dp', 'slot')
- grad_up: float32 [512, 2048], P('dp', 'slot')
- grad_down: float32 [2048, 512], P('slot', 'dp')
- grad_gain_attn: float32 [512], P(('dp', 'slot'))
- grad_gain_ffn: float32 [512], P(('dp', 'slot'))
Inputs may be any that keep to these rules, and one draw needn't show every extreme that they name: A 1 starts a new document at that position; documents never cross rows.
All inputs are finite; a program needn't handle non-finite values. No bound on the sum of `starts` on one device may be relied on, other than what follows from the above.
Results may differ from a plain program's by a relative error of at most 0.022.
Values may be sent and summed in bfloat16 or wider, within the bound.
A program may use at most 192 MiB of HBM per device.

v0:
```python
import jax
import jax.numpy as jnp
from jax import lax
from jax.sharding import PartitionSpec as P

HEADS = 8


EPSILON = 1e-05
NARROW = jnp.bfloat16
WIDE = jnp.float32


def as_low(value):
    return value.astype(NARROW)


def rounded(value):
    return value.astype(NARROW).astype(WIDE)


def einsum_wide(pattern, first_op, second_op):
    return jnp.einsum(pattern, first_op, second_op, preferred_element_type=WIDE)


def gelu_exact(values):
    return jax.nn.gelu(values, approximate=False)


def norm_parts(values):
    center = values - jnp.mean(values, axis=-1, keepdims=True)
    inv_scale = lax.rsqrt(jnp.mean(center * center, axis=-1, keepdims=True) + EPSILON)
    return (center * inv_scale, inv_scale)


def norm_back(normed, inv_scale, gain_row, upstream):
    grad_hat = upstream * gain_row
    centered = grad_hat - jnp.mean(grad_hat, axis=-1, keepdims=True)
    return (centered - normed * jnp.mean(grad_hat * normed, axis=-1, keepdims=True)) * inv_scale


def visibility(starts):
    segment = jnp.cumsum(starts, axis=1)
    places = jnp.arange(starts.shape[1], dtype=jnp.int32)
    allowed = (places[None, None, :] <= places[None, :, None]) & (
        segment[:, None, :] == segment[:, :, None]
    )
    return allowed.astype(NARROW)


def split_heads(flat_rows, row_count, length):
    return flat_rows.reshape(row_count, length, HEADS, -1).transpose(2, 0, 1, 3)


def join_heads(stacked):
    return stacked.transpose(1, 2, 0, 3).reshape(-1, stacked.shape[0] * stacked.shape[3])


def split_slots(flat_rows, row_count, length):
    return flat_rows.reshape(row_count, length, -1, HEADS).transpose(3, 0, 1, 2)


def join_slots(stacked):
    return stacked.transpose(1, 2, 3, 0).reshape(-1, stacked.shape[3] * stacked.shape[0])


def attention_inputs(
    flat_rows, gain_one, full_query, full_key, full_value, slot_w, row_count, length
):
    normed_one, scale_one = norm_parts(flat_rows)
    normed_low = as_low(normed_one * gain_one)
    query_rows = split_heads(
        as_low(jnp.dot(normed_low, full_query, preferred_element_type=WIDE)), row_count, length
    )
    key_matrix = split_heads(
        as_low(jnp.dot(normed_low, full_key, preferred_element_type=WIDE)), row_count, length
    )
    value_matrix = split_heads(
        as_low(jnp.dot(normed_low, full_value, preferred_element_type=WIDE)), row_count, length
    )
    logits = jnp.dot(normed_low, slot_w, preferred_element_type=WIDE)
    slot_weight = split_slots(as_low(jnp.exp(logits)), row_count, length)
    return (
        normed_one,
        scale_one,
        normed_low,
        query_rows,
        key_matrix,
        value_matrix,
        logits,
        slot_weight,
    )


def ffn_pass(middle_rows_in, grad_rows_in, gain_two, up_w, down_w):
    normed_two, scale_two = norm_parts(middle_rows_in)
    second_low = as_low(normed_two * gain_two)
    hidden = jnp.dot(second_low, up_w, preferred_element_type=WIDE)
    active = as_low(gelu_exact(hidden))
    branch = jnp.dot(active, down_w, preferred_element_type=WIDE)
    grad_low = as_low(grad_rows_in)
    grad_down = einsum_wide("tf,td->fd", active, grad_low)
    grad_active = einsum_wide("td,fd->tf", grad_low, down_w)
    gelu_value, gelu_pull = jax.vjp(gelu_exact, hidden)
    grad_hidden = as_low(gelu_pull(grad_active)[0])
    grad_up = einsum_wide("td,tf->df", second_low, grad_hidden)
    grad_second_part = einsum_wide("tf,df->td", grad_hidden, up_w)
    return (branch, normed_two, scale_two, grad_up, grad_down, grad_second_part)


def on_device(
    inputs,
    starts,
    w_query,
    w_key,
    w_value,
    w_out,
    w_slot,
    w_up,
    w_down,
    gain_attn,
    gain_ffn,
    cotangent,
):
    full_query, full_key, full_value, full_out, gain_first, gain_second = (
        lax.all_gather(w_query, ("dp", "slot"), axis=0, tiled=True),
        lax.all_gather(w_key, ("dp", "slot"), axis=0, tiled=True),
        lax.all_gather(w_value, ("dp", "slot"), axis=0, tiled=True),
        lax.all_gather(w_out, ("dp", "slot"), axis=0, tiled=True),
        lax.all_gather(gain_attn, ("dp", "slot"), axis=0, tiled=True),
        lax.all_gather(gain_ffn, ("dp", "slot"), axis=0, tiled=True),
    )
    slot_w, up_w, down_w = (
        lax.all_gather(w_slot, "dp", axis=0, tiled=True),
        lax.all_gather(w_up, "dp", axis=0, tiled=True),
        lax.all_gather(w_down, "dp", axis=1, tiled=True),
    )
    gain_one = gain_first.astype(WIDE)
    gain_two = gain_second.astype(WIDE)
    row_count, length, model_width = inputs.shape
    tokens = row_count * length
    flat_rows = inputs.reshape(tokens, model_width)
    grad_flat = cotangent.reshape(tokens, model_width)
    visible = visibility(starts)
    slot_count = lax.axis_size("slot")
    quarter = tokens // slot_count
    own_start = lax.axis_index("slot") * quarter

    def own_rows(values):
        return lax.dynamic_slice_in_dim(values, own_start, quarter, 0)

    def head_scores(pieces):
        query_h, key_h, weight_h = pieces
        cross_low = as_low(visible * einsum_wide("rld,rmd->rlm", query_h, key_h))
        return einsum_wide("rlm,rmc->rlc", cross_low, weight_h)

    def head_mix(pieces):
        scaled_h, weight_h, value_h = pieces
        mixture_narrow = as_low(visible * einsum_wide("rlc,rmc->rlm", scaled_h, weight_h))
        return einsum_wide("rlm,rmd->rld", mixture_narrow, value_h)

    def head_back_mix(pieces):
        scaled_h, weight_h, value_h, grad_h = pieces
        mixture_narrow = as_low(visible * einsum_wide("rlc,rmc->rlm", scaled_h, weight_h))
        grad_mix = as_low(visible * einsum_wide("rld,rmd->rlm", grad_h, value_h))
        return (
            einsum_wide("rlm,rld->rmd", mixture_narrow, grad_h),
            einsum_wide("rlm,rmc->rlc", grad_mix, weight_h),
            einsum_wide("rlm,rlc->rmc", grad_mix, scaled_h),
        )

    def head_back_score(pieces):
        query_h, key_h, weight_h, grad_h = pieces
        cross_low = as_low(visible * einsum_wide("rld,rmd->rlm", query_h, key_h))
        grad_cross = as_low(visible * einsum_wide("rlc,rmc->rlm", grad_h, weight_h))
        return (
            einsum_wide("rlm,rmd->rld", grad_cross, key_h),
            einsum_wide("rlm,rld->rmd", grad_cross, query_h),
            einsum_wide("rlm,rlc->rmc", cross_low, grad_h),
        )

    first_pass = attention_inputs(
        flat_rows, gain_one, full_query, full_key, full_value, slot_w, row_count, length
    )
    slot_weight = first_pass[7]
    totals = einsum_wide("rlm,hrmc->hrlc", visible, slot_weight)
    slot_score = lax.map(head_scores, (first_pass[3], first_pass[4], slot_weight)) / totals
    local_top = jnp.max(slot_score, axis=-1)
    slot_top = lax.pmax(local_top, "slot")
    shifted = jnp.exp(slot_score - slot_top[..., None])
    slot_denom = lax.psum(jnp.sum(shifted, axis=-1), "slot")
    slot_prob = shifted / slot_denom[..., None]
    scaled_low = as_low(slot_prob / totals)
    partial_out = join_heads(lax.map(head_mix, (scaled_low, slot_weight, first_pass[5])))
    merged_low = as_low(lax.psum(partial_out, "slot"))
    middle = flat_rows + jnp.dot(merged_low, full_out, preferred_element_type=WIDE)
    branch, normed_two, scale_two, grad_up, grad_down, grad_part = ffn_pass(
        middle, grad_flat, gain_two, up_w, down_w
    )
    output = middle + lax.psum(branch, "slot")
    grad_second = lax.psum(grad_part, "slot")
    grad_middle = grad_flat + norm_back(normed_two, scale_two, gain_two, grad_second)
    grad_gain_two = jnp.sum(own_rows(grad_second * normed_two), axis=0)
    merged_mine = own_rows(merged_low)
    grad_attn_low = as_low(grad_middle)
    grad_out_w = einsum_wide("td,te->de", merged_mine, own_rows(grad_attn_low))
    grad_merged = split_heads(
        as_low(einsum_wide("te,de->td", grad_attn_low, full_out)), row_count, length
    )
    normed_one, scale_one, normed_low, query_rows, key_matrix, value_matrix, logits, slot_again = (
        attention_inputs(
            flat_rows, gain_one, full_query, full_key, full_value, slot_w, row_count, length
        )
    )
    grad_value_h, grad_scaled, grad_weight_mix = lax.map(
        head_back_mix, (scaled_low, slot_again, value_matrix, grad_merged)
    )
    grad_scaled = rounded(grad_scaled)
    grad_prob = grad_scaled / totals
    inner_sum = lax.psum(jnp.sum(slot_prob * grad_prob, axis=-1), "slot")
    grad_score = slot_prob * (grad_prob - inner_sum[..., None])
    grad_totals = as_low(-(grad_scaled * slot_prob / totals + grad_score * slot_score) / totals)
    grad_numer = as_low(grad_score / totals)
    grad_query_h, grad_key_h, grad_weight_score = lax.map(
        head_back_score, (query_rows, key_matrix, slot_again, grad_numer)
    )
    grad_weight_total = (
        grad_weight_mix + grad_weight_score + einsum_wide("rlm,hrlc->hrmc", visible, grad_totals)
    )
    exact_weight = jnp.exp(split_slots(logits, row_count, length))
    grad_logits = join_slots(as_low(rounded(grad_weight_total) * exact_weight))
    grad_slot_w = einsum_wide("td,tc->dc", normed_low, grad_logits)
    grad_cross_in = einsum_wide("tc,dc->td", grad_logits, slot_w)
    grad_heads = (
        join_heads(grad_query_h),
        join_heads(grad_key_h),
        join_heads(grad_value_h),
        grad_cross_in,
    )
    summed = lax.psum((grad_heads[0], grad_heads[1], grad_heads[2], grad_heads[3]), "slot")
    query_low = as_low(summed[0])
    key_low = as_low(summed[1])
    value_low = as_low(summed[2])
    grad_first = (
        summed[3]
        + einsum_wide("te,de->td", query_low, full_query)
        + einsum_wide("te,de->td", key_low, full_key)
        + einsum_wide("te,de->td", value_low, full_value)
    )
    full_lows, grad_first = ((query_low, key_low, value_low), grad_first)
    grad_inputs = grad_middle + norm_back(normed_one, scale_one, gain_one, grad_first)
    low_grads = tuple((own_rows(member) for member in full_lows))
    own_first = own_rows(grad_first)
    own_normed = own_rows(normed_low)
    grad_query_w = einsum_wide("td,te->de", own_normed, low_grads[0])
    grad_key_w = einsum_wide("td,te->de", own_normed, low_grads[1])
    grad_value_w = einsum_wide("td,te->de", own_normed, low_grads[2])
    grad_gain_one = jnp.sum(own_first * own_rows(normed_one), axis=0)
    grad_slot_part, grad_up_part, grad_down_part = (
        lax.psum_scatter(grad_slot_w, "dp", scatter_dimension=0, tiled=True),
        lax.psum_scatter(grad_up, "dp", scatter_dimension=0, tiled=True),
        lax.psum_scatter(grad_down, "dp", scatter_dimension=1, tiled=True),
    )
    dense_grads = (
        lax.psum_scatter(grad_query_w, ("dp", "slot"), scatter_dimension=0, tiled=True),
        lax.psum_scatter(grad_key_w, ("dp", "slot"), scatter_dimension=0, tiled=True),
        lax.psum_scatter(grad_value_w, ("dp", "slot"), scatter_dimension=0, tiled=True),
        lax.psum_scatter(grad_out_w, ("dp", "slot"), scatter_dimension=0, tiled=True),
        lax.psum_scatter(grad_gain_one, ("dp", "slot"), scatter_dimension=0, tiled=True),
        lax.psum_scatter(grad_gain_two, ("dp", "slot"), scatter_dimension=0, tiled=True),
    )
    return (
        output.reshape(row_count, length, model_width),
        grad_inputs.reshape(row_count, length, model_width),
        dense_grads[0],
        dense_grads[1],
        dense_grads[2],
        dense_grads[3],
        grad_slot_part,
        grad_up_part,
        grad_down_part,
        dense_grads[4],
        dense_grads[5],
    )


def solution(mesh):
    placed = (
        P("dp", None, None),
        P("dp", None),
        P(("dp", "slot"), None),
        P(("dp", "slot"), None),
        P(("dp", "slot"), None),
        P(("dp", "slot"), None),
        P("dp", "slot"),
        P("dp", "slot"),
        P("slot", "dp"),
        P(("dp", "slot")),
        P(("dp", "slot")),
        P("dp", None, None),
    )
    return jax.shard_map(
        on_device,
        mesh=mesh,
        in_specs=placed,
        out_specs=(
            P("dp", None, None),
            P("dp", None, None),
            P(("dp", "slot"), None),
            P(("dp", "slot"), None),
            P(("dp", "slot"), None),
            P(("dp", "slot"), None),
            P("dp", "slot"),
            P("dp", "slot"),
            P("slot", "dp"),
            P(("dp", "slot")),
            P(("dp", "slot")),
        ),
        check_vma=False,
    )
```

profile of v0, /device:TPU:0, one launch (start us, length us, event | category | flops | bytes accessed | tf_op | source)
XLA Modules:
  0.0 1960.6 jit_solution(8838840183732900454)
XLA Ops:
  10.2 42.0 %all-reduce.7 = (bf16[512]{0:T(512)(128)(2,1)S(1)}, bf16[512]{0:T(512)(128)(2,1)S(1)}) all-reduce(bf16[512]{0:T(512)(128)(2,1)S(1)} %dynamic-update-slice, bf16[512]{0:T(512)(128)(2,1)S(1)} %dynamic-update-slice.1), channel_id=1, replica_groups=mesh['dp'=8,'slot'=4] {'dp','slot'}, use_global_device_ids=true, to_apply=%add | all-reduce | flops 1024 | bytes 4096
  60.3 30.6 %all_gather.30 = bf16[512,128]{1,0:T(8,128)(2,1)S(1)} all-gather(bf16[64,128]{1,0:T(8,128)(2,1)S(1)} %copy-done.46), channel_id=1, replica_groups=mesh['dp'=8,'slot'=4] {'dp'}, dimensions={0}, use_global_device_ids=true | all-gather | bytes 147456 | tf_op jit(solution)/shard_map/all_gather | solution.py:134
  90.9 41.6 %all_gather.28 = bf16[512,512]{1,0:T(8,128)(2,1)S(1)} all-gather(bf16[16,512]{1,0:T(8,128)(2,1)S(1)} %copy-done.47), channel_id=1, replica_groups=mesh['dp'=8,'slot'=4] {'dp','slot'}, dimensions={0}, use_global_device_ids=true | all-gather | bytes 540672 | tf_op jit(solution)/shard_map/all_gather | solution.py:126
  132.5 38.2 %all_gather.29 = bf16[512,512]{1,0:T(8,128)(2,1)S(1)} all-gather(bf16[16,512]{1,0:T(8,128)(2,1)S(1)} %copy-done.48), channel_id=1, replica_groups=mesh['dp'=8,'slot'=4] {'dp','slot'}, dimensions={0}, use_global_device_ids=true | all-gather | bytes 540672 | tf_op jit(solution)/shard_map/all_gather | solution.py:127
  211.9 37.9 %while.52 = (s32[]{:T(128)}, f32[8,2,1024,16]{2,3,0,1:T(8,128)}, bf16[8,2,1024,64]{2,3,1,0:T(8,128)(2,1)}, bf16[8,2,1024,64]{2,3,1,0:T(8,128)(2,1)}, bf16[8,2,10...) while((s32[]{:T(128)}, f32[8,2,1024,16]{2,3,0,1:T(8,128)}, ...), condition=%wide.region_5.6_spmd.clone, body=%wide.region_4.5_spmd.clone.sunk | while | flops 348127232 | bytes 1787997 | solution.py:187
  211.9 4.7 fusion.276
  216.6 4.7 fusion.276
  221.3 4.7 fusion.276
  235.5 4.7 fusion.276
  245.0 4.7 fusion.276
  249.7 5.9 fusion.192
  255.8 39.4 %all_gather.31 = bf16[512,512]{1,0:T(8,128)(2,1)S(1)} all-gather(bf16[16,512]{1,0:T(8,128)(2,1)S(1)} %copy-done.49), channel_id=1, replica_groups=mesh['dp'=8,'slot'=4] {'dp','slot'}, dimensions={0}, use_global_device_ids=true | all-gather | bytes 540672 | tf_op jit(solution)/shard_map/all_gather | solution.py:128
  295.2 40.9 %all_gather.32 = bf16[512,512]{1,0:T(8,128)(2,1)} all-gather(bf16[16,512]{1,0:T(8,128)(2,1)S(1)} %copy-done.50), channel_id=1, replica_groups=mesh['dp'=8,'slot'=4] {'dp','slot'}, dimensions={0}, use_global_device_ids=true | all-gather | bytes 540672 | tf_op jit(solution)/shard_map/all_gather | solution.py:129
  342.5 33.4 %all_gather.34 = bf16[512,512]{1,0:T(8,128)(2,1)} all-gather(bf16[64,512]{1,0:T(8,128)(2,1)S(1)} %copy-done.40), channel_id=1, replica_groups=mesh['dp'=8,'slot'=4] {'dp'}, dimensions={0}, use_global_device_ids=true | all-gather | bytes 589824 | tf_op jit(solution)/shard_map/all_gather | solution.py:135
  377.7 33.4 %all_gather.35 = bf16[512,512]{0,1:T(8,128)(2,1)} all-gather(bf16[512,64]{0,1:T(8,128)(2,1)S(1)} %copy-done.41), channel_id=1, replica_groups=mesh['dp'=8,'slot'=4] {'dp'}, dimensions={1}, use_global_device_ids=true | all-gather | bytes 589824 | tf_op jit(solution)/shard_map/all_gather | solution.py:136
  427.0 42.5 %while.53 = (s32[]{:T(128)}, f32[8,2,1024,64]{2,3,1,0:T(8,128)}, bf16[8,2,1024,16]{2,3,1,0:T(8,128)(2,1)S(1)}, bf16[8,2,1024,16]{2,3,1,0:T(8,128)(2,1)}, bf16[8,...) while((s32[]{:T(128)}, f32[8,2,1024,64]{2,3,1,0:T(8,128)}, ...), condition=%wide.region_11.12_spmd.clone, body=%wide.region_10.11_spmd.clone.sunk | while | flops 348127232 | bytes 1984605 | solution.py:194
  427.0 5.3 fusion.280
  432.3 5.3 fusion.280
  437.6 5.3 fusion.280
  442.9 5.3 fusion.280
  448.2 5.3 fusion.280
  453.5 5.3 fusion.280
  458.8 5.3 fusion.280
  464.1 5.3 fusion.280
  469.4 5.6 copy.82
  479.0 76.5 %all-reduce.25 = bf16[2048,512]{0,1:T(8,128)(2,1)S(1)} all-reduce(f32[2048,512]{0,1:T(8,128)} %bitcast.337), channel_id=1, replica_groups=mesh['dp'=8,'slot'=4] {'slot'}, use_global_device_ids=true, to_apply=%region_12.13 | all-reduce | flops 1048576 | bytes 6291456 | tf_op jit(solution)/shard_map/psum | solution.py:195
  565.6 11.7 add_convert_fusion
  590.8 74.6 %all-reduce.20.cloned.1.call-done = f32[2048,512]{1,0:T(8,128)} async-done(((f32[2048,512]{1,0:T(8,128)}), f32[2048,512]{1,0:T(8,128)}) %all-reduce.20.cloned.1.call-update) | async-done | bytes 4194320 | tf_op jit(solution)/shard_map/psum | solution.py:201
  665.3 4.8 multiply_reduce_fusion.5
  671.3 6.2 fusion.190
  693.4 116.0 %while.54 = (s32[]{:T(128)}, f32[8,2,1024,64]{2,3,1,0:T(8,128)}, bf16[8,2,1024,16]{2,3,0,1:T(8,128)(2,1)}, f32[8,2,1024,16]{2,3,0,1:T(8,128)}, bf16[8,2,1024,16]...) while((s32[]{:T(128)}, f32[8,2,1024,64]{2,3,1,0:T(8,128)}, ...), condition=%wide.region_20.21_spmd.clone, body=%wide.region_19.20_spmd.clone.sunk | while | flops 763363328 | bytes 17075836 | solution.py:215
  703.0 5.0 fusion.289
  717.5 5.0 fusion.289
  732.0 5.0 fusion.289
  746.5 5.0 fusion.289
  760.9 5.0 fusion.289
  775.4 5.0 fusion.289
  789.9 5.0 fusion.289
  804.4 5.0 fusion.289
  816.4 27.0 %all-reduce.22.cloned.1.call-done = f32[8,2,1024]{2,0,1:T(8,128)} async-done(((f32[8,2,1024]{2,0,1:T(8,128)}), f32[8,2,1024]{2,0,1:T(8,128)}) %all-reduce.22.cloned.1.call-update) | async-done | bytes 65552 | tf_op jit(solution)/shard_map/psum | solution.py:220
  852.2 112.3 %while.55 = (s32[]{:T(128)}, f32[8,2,1024,64]{2,3,1,0:T(8,128)}, f32[8,2,1024,64]{2,3,1,0:T(8,128)}, f32[8,2,1024,16]{2,3,0,1:T(8,128)}, bf16[8,2,1024,16]{2,3,0...) while((s32[]{:T(128)}, f32[8,2,1024,64]{2,3,1,0:T(8,128)}, ...), condition=%wide.region_24.25_spmd.clone, body=%wide.region_23.24_spmd.clone.sunk | while | flops 964689920 | bytes 17142900 | solution.py:224
  852.4 4.8 fusion.306
  866.5 4.8 fusion.306
  880.5 4.8 fusion.306
  894.6 4.8 fusion.306
  908.5 4.8 fusion.306
  922.6 4.8 fusion.306
  936.5 4.8 fusion.306
  950.6 4.8 fusion.306
  964.6 5.7 fusion.154
  978.2 5.9 fusion.165
  988.4 5.4 copy.100
  1000.6 5.5 copy.98
  1017.3 307.0 %all-reduce.26 = (bf16[2048,512]{0,1:T(8,128)(2,1)}, bf16[2048,512]{0,1:T(8,128)(2,1)}, bf16[2048,512]{0,1:T(8,128)(2,1)}) all-reduce(f32[2048,512]{0,1:T(8,128)} %bitcast.331, f32[2048,512]{0,1:T(8,128)} %bitcast.330, f32[2048,512]{0,1:T(8,128)} %bitcast.329), channel_id=1, replica_groups=mesh['dp'=8,'slot'=4] {'slot'}, use_global_device_ids=true, to_apply=%region_27.28 | all-reduce | flops 3145728 | bytes 18874368 | tf_op jit(solution)/shard_map/psum | solution.py:240
  1333.9 5.0 fusion.199
  1342.3 6.8 add.111
  1350.9 5.4 multiply_reduce_fusion.4
  1358.5 39.7 %all-reduce.4 = (f32[512]{0:T(512)S(1)}, f32[512]{0:T(512)S(1)}) all-reduce(f32[512]{0:T(512)S(1)} %multiply_reduce_fusion.6, f32[512]{0:T(512)S(1)} %fusion.161), channel_id=9, replica_groups=mesh['dp'=8,'slot'=4] {'dp','slot'}, use_global_device_ids=true, to_apply=%region_39.40.clone | all-reduce | flops 1024 | bytes 8192
  1399.3 7.2 multiply_add_fusion
  1406.5 9.8 reduce-scatter.16.cloned.1.call-done
  1416.4 136.7 %reduce-scatter.14.cloned.1.call-done = f32[16,512]{1,0:T(8,128)} async-done(((f32[512,512]{1,0:T(8,128)}), f32[16,512]{1,0:T(8,128)}) %reduce-scatter.14.cloned.1.call-update) | async-done | bytes 32784 | tf_op jit(solution)/shard_map/reduce_scatter | solution.py:268
  1553.0 133.5 %reduce-scatter.10.cloned.1.call-done = f32[16,512]{1,0:T(8,128)} async-done(((f32[512,512]{1,0:T(8,128)}), f32[16,512]{1,0:T(8,128)}) %reduce-scatter.10.cloned.1.call-update) | async-done | bytes 32784 | tf_op jit(solution)/shard_map/reduce_scatter | solution.py:266
  1686.5 133.5 %reduce-scatter.12.cloned.1.call-done = f32[16,512]{1,0:T(8,128)} async-done(((f32[512,512]{1,0:T(8,128)}), f32[16,512]{1,0:T(8,128)}) %reduce-scatter.12.cloned.1.call-update) | async-done | bytes 32784 | tf_op jit(solution)/shard_map/reduce_scatter | solution.py:267
  1820.0 133.5 %reduce-scatter.8.cloned.1.call-done = f32[16,512]{1,0:T(8,128)} async-done(((f32[512,512]{1,0:T(8,128)}), f32[16,512]{1,0:T(8,128)}) %reduce-scatter.8.cloned.1.call-update) | async-done | bytes 32784 | tf_op jit(solution)/shard_map/reduce_scatter | solution.py:265
  (277 shorter events, 348.6 us)
Async XLA Ops:
  7.2 368.7 %all-reduce.16.cloned.1.call-start = ((), (), s32[]{:S(2)}) async-start(), calls=%async_computation.7 | async-start | bytes 131072 | tf_op jit(solution)/shard_map/pmax | solution.py:189
  52.2 118.5 %copy-start.43 = (f32[512]{0:T(512)}, f32[512]{0:T(512)S(1)}, u32[]{:S(2)}) copy-start(f32[512]{0:T(512)S(1)} %convert_element_type.121) | copy-start | bytes 6148
  54.0 6.3 copy-start.46
  54.0 36.9 %copy-start.47 = (bf16[16,512]{1,0:T(8,128)(2,1)S(1)}, bf16[16,512]{1,0:T(8,128)(2,1)}, u32[]{:S(2)}) copy-start(bf16[16,512]{1,0:T(8,128)(2,1)} %param.22) | copy-start | bytes 49156
  54.0 78.5 %copy-start.48 = (bf16[16,512]{1,0:T(8,128)(2,1)S(1)}, bf16[16,512]{1,0:T(8,128)(2,1)}, u32[]{:S(2)}) copy-start(bf16[16,512]{1,0:T(8,128)(2,1)} %param.23) | copy-start | bytes 49156
  56.6 114.1 %copy-start.2 = (f32[2,1024,512]{2,1,0:T(8,128)S(1)}, f32[2,1024,512]{2,1,0:T(8,128)}, u32[]{:S(2)}) copy-start(f32[2,1024,512]{2,1,0:T(8,128)} %param.20) | copy-start | bytes 12582916
  56.6 116.7 %copy-start.36 = (f32[2,1024]{1,0:T(2,128)}, f32[2,1024]{1,0:T(2,128)S(1)}, u32[]{:S(2)}) copy-start(f32[2,1024]{1,0:T(2,128)S(1)} %get-tuple-element.459) | copy-start | bytes 24580
  60.3 113.1 %copy-start.38 = (f32[1,8,2,128]{3,1,2,0:T(8,128)}, f32[1,8,2,128]{3,1,2,0:T(8,128)S(1)}, u32[]{:S(2)}) copy-start(f32[1,8,2,128]{3,1,2,0:T(8,128)S(1)} %copy.149) | copy-start | bytes 24580
  90.9 82.5 %copy-start.31 = (bf16[512,128]{1,0:T(8,128)(2,1)}, bf16[512,128]{1,0:T(8,128)(2,1)S(1)}, u32[]{:S(2)}) copy-start(bf16[512,128]{1,0:T(8,128)(2,1)S(1)} %all_gather.30) | copy-start | bytes 393220
  132.5 63.7 %copy-start.24 = (bf16[512,512]{1,0:T(8,128)(2,1)}, bf16[512,512]{1,0:T(8,128)(2,1)S(1)}, u32[]{:S(2)}) copy-start(bf16[512,512]{1,0:T(8,128)(2,1)S(1)} %all_gather.28) | copy-start | bytes 1572868
  170.7 11.0 copy-start.22
  173.3 166.6 %copy-start.12 = (bf16[2048,512]{1,0:T(8,128)(2,1)}, bf16[2048,512]{1,0:T(8,128)(2,1)S(1)}, u32[]{:S(2)}) copy-start(bf16[2048,512]{1,0:T(8,128)(2,1)S(1)} %get-tuple-element.454) | copy-start | bytes 6291460
  202.7 9.2 copy-start.34
  249.7 6.0 copy-start.49
  249.7 45.5 %copy-start.50 = (bf16[16,512]{1,0:T(8,128)(2,1)S(1)}, bf16[16,512]{1,0:T(8,128)(2,1)}, u32[]{:S(2)}) copy-start(bf16[16,512]{1,0:T(8,128)(2,1)} %param.25) | copy-start | bytes 49156
  255.7 167.5 %all-reduce.18.cloned.1.call-start = ((), (), s32[]{:S(2)}) async-start(), calls=%async_computation.8 | async-start | bytes 131072 | tf_op jit(solution)/shard_map/psum | solution.py:191
  295.2 47.3 %copy-start.26 = (bf16[512,512]{1,0:T(8,128)(2,1)}, bf16[512,512]{1,0:T(8,128)(2,1)S(1)}, u32[]{:S(2)}) copy-start(bf16[512,512]{1,0:T(8,128)(2,1)S(1)} %all_gather.31) | copy-start | bytes 1572868
  339.9 2.6 copy-start.40
  339.9 37.8 %copy-start.41 = (bf16[512,64]{0,1:T(8,128)(2,1)S(1)}, bf16[512,64]{0,1:T(8,128)(2,1)}, u32[]{:S(2)}) copy-start(bf16[512,64]{0,1:T(8,128)(2,1)} %param.28) | copy-start | bytes 196612
  377.7 287.7 %all-reduce.20.cloned.1.call-start = ((), (), s32[]{:S(2)}) async-start(), calls=%async_computation.9 | async-start | bytes 8388608 | tf_op jit(solution)/shard_map/psum | solution.py:201
  415.0 8.2 copy-start.15
  415.0 8.2 copy-start.33
  469.4 5.6 copy-start.30
  555.5 4.6 copy-start.10
  560.1 2.0 copy-start
  561.0 1.4 copy-start.17
  562.4 2.1 copy-start.3
  562.4 3.1 copy-start.21
  562.4 3.2 copy-start.28
  565.6 11.7 copy-start.5
  577.3 1.3 copy-start.14
  581.9 1.2 copy-start.18
  581.9 261.4 %all-reduce.22.cloned.1.call-start = ((), (), s32[]{:S(2)}) async-start(), calls=%async_computation.10 | async-start | bytes 131072 | tf_op jit(solution)/shard_map/psum | solution.py:220
  665.3 4.8 copy-start.1
  665.3 5.9 copy-start.8
  671.3 7.5 copy-start.29
  677.5 1.3 copy-start.19
  693.4 116.0 %copy-start.35 = (f32[8,2,1024]{2,0,1:T(8,128)S(1)}, f32[8,2,1024]{2,0,1:T(8,128)}, u32[]{:S(2)}) copy-start(f32[8,2,1024]{2,0,1:T(8,128)} %all-reduce.18.cloned.1.call-done) | copy-start | bytes 196612
  812.0 530.2 %all-reduce.24.cloned.1.call-start = ((), (), s32[]{:S(2)}) async-start(), calls=%async_computation.18 | async-start | bytes 16777216 | tf_op jit(solution)/shard_map/psum | solution.py:200
  852.2 112.3 %copy-start.42 = (f32[8,2,1024]{2,0,1:T(8,128)S(1)}, f32[8,2,1024]{2,0,1:T(8,128)}, u32[]{:S(2)}) copy-start(f32[8,2,1024]{2,0,1:T(8,128)} %all-reduce.22.cloned.1.call-done) | copy-start | bytes 196612
  964.6 6.4 copy-start.32
  973.7 432.8 %reduce-scatter.20.cloned.1.call-start = ((), (), s32[]{:S(2)}) async-start(), calls=%async_computation.17 | async-start | bytes 1179648 | tf_op jit(solution)/shard_map/reduce_scatter | solution.py:262
  977.7 6.5 copy-start.37
  977.7 6.5 copy-start.44
  977.7 6.5 copy-start.45
  977.7 428.8 %reduce-scatter.18.cloned.1.call-start = ((), (), s32[]{:S(2)}) async-start(), calls=%async_computation.16 | async-start | bytes 1179648 | tf_op jit(solution)/shard_map/reduce_scatter | solution.py:261
  984.1 432.2 %reduce-scatter.16.cloned.1.call-start = ((), (), s32[]{:S(2)}) async-start(), calls=%async_computation.15 | async-start | bytes 294912 | tf_op jit(solution)/shard_map/reduce_scatter | solution.py:260
  988.4 564.6 %reduce-scatter.14.cloned.1.call-start = ((), (), s32[]{:S(2)}) async-start(), calls=%async_computation.14 | async-start | bytes 1081344 | tf_op jit(solution)/shard_map/reduce_scatter | solution.py:268
  1000.4 686.1 %reduce-scatter.10.cloned.1.call-start = ((), (), s32[]{:S(2)}) async-start(), calls=%async_computation.12 | async-start | bytes 1081344 | tf_op jit(solution)/shard_map/reduce_scatter | solution.py:266
  1006.1 4.1 copy-start.11
  1017.3 307.0 %copy-start.13 = (bf16[2048,512]{1,0:T(8,128)(2,1)S(1)}, bf16[2048,512]{1,0:T(8,128)(2,1)}, u32[]{:S(2)}) copy-start(bf16[2048,512]{1,0:T(8,128)(2,1)} %copy-done.12) | copy-start | bytes 6291460
  1326.8 7.0 copy-start.25
  1326.9 493.1 %reduce-scatter.12.cloned.1.call-start = ((), (), s32[]{:S(2)}) async-start(), calls=%async_computation.13 | async-start | bytes 1081344 | tf_op jit(solution)/shard_map/reduce_scatter | solution.py:267
  1329.5 624.0 %reduce-scatter.8.cloned.1.call-start = ((), (), s32[]{:S(2)}) async-start(), calls=%async_computation.11 | async-start | bytes 1081344 | tf_op jit(solution)/shard_map/reduce_scatter | solution.py:265
  1333.9 5.0 copy-start.16
  1333.9 5.0 copy-start.23
  1338.9 10.2 copy-start.20
  1338.9 10.2 copy-start.27
  1342.2 6.9 copy-start.4
  1342.2 6.9 copy-start.6
  1342.2 8.7 copy-start.7
  1350.9 48.4 %copy-start.39 = (f32[1,8,2,128]{3,1,2,0:T(8,128)S(1)}, f32[1,8,2,128]{3,1,2,0:T(8,128)}, u32[]{:S(2)}) copy-start(f32[1,8,2,128]{3,1,2,0:T(8,128)} %copy-done.38) | copy-start | bytes 24580
  1356.3 2.0 copy-start.9
Sparse Core Ops, SparseCore 0:
  255.8 28.7 all-reduce.15
  377.8 28.9 all-reduce.17
  582.0 83.2 all-reduce.19
  812.1 31.2 all-reduce.21
  973.8 244.0 all-reduce.23
  1221.7 63.5 reduce-scatter.19
  1289.6 62.5 reduce-scatter.17
  1356.1 60.2 reduce-scatter.15
  1419.2 133.7 reduce-scatter.13
  1555.8 130.6 reduce-scatter.9
  1689.3 130.6 reduce-scatter.11
  1822.8 130.6 reduce-scatter.7
where the time goes:
time: 1970 us; the launch traced here: 1960 us
  blocking collectives  723 us (37%)
  waiting for transfers between devices  649 us (33%)
  matrix products  386 us (20%)
  local copies, waits for them, and re-layouts  127 us (6%)
  other arithmetic  59.4 us (3%)
    dot_general x96, matrix products, einsum_wide(): return jnp.einsum(pattern, first_op, second_op, preferred_element_type=WIDE)  366 us
    psum x1, blocking collectives, on_device(): lax.psum((grad_heads[0], grad_heads[1], grad_heads[2], grad_heads[3]), 's...  307 us
    reduce_scatter x1, waiting for transfers between devices, on_device(): lax.psum_scatter(grad_out_w, ('dp', 'slot'), scatter_dimension=0, tiled=T...  137 us
    reduce_scatter x1, waiting for transfers between devices, on_device(): lax.psum_scatter(grad_value_w, ('dp', 'slot'), scatter_dimension=0, tiled...  134 us
    reduce_scatter x1, waiting for transfers between devices, on_device(): lax.psum_scatter(grad_query_w, ('dp', 'slot'), scatter_dimension=0, tiled...  133 us
    reduce_scatter x1, waiting for transfers between devices, on_device(): lax.psum_scatter(grad_key_w, ('dp', 'slot'), scatter_dimension=0, tiled=T...  133 us
    unnamed x2, blocking collectives  81.7 us
    psum x1, blocking collectives, on_device(): merged_low = as_low(lax.psum(partial_out, 'slot'))  76.5 us
  transfers between devices with their start and end apart: 12, of which 7 were waited for; matrix products, arithmetic and copies ran while one was open for 6% of the time, Pallas kernels for 0%

commit v1 on v0

v1 whole, which is shorter than its diff:
```python
import functools

import jax
import jax.numpy as jnp
from jax import lax
from jax.experimental import pallas as pl
from jax.experimental.pallas import tpu as pltpu
from jax.sharding import PartitionSpec as P

HEADS = 8
EPSILON = 1e-05
NARROW = jnp.bfloat16
WIDE = jnp.float32
MESH = pl.DeviceIdType.MESH

WIDTH = 512
CHUNK = 128
PAIRS = 4
LANES = 128
EARLY = 272
LATE = 576


def dot(a, b):
    return lax.dot_general(a, b, (((1,), (0,)), ((), ())), preferred_element_type=WIDE)


def dot_nt(a, b):
    return lax.dot_general(a, b, (((1,), (1,)), ((), ())), preferred_element_type=WIDE)


def dot_tn(a, b):
    return lax.dot_general(a, b, (((0,), (0,)), ((), ())), preferred_element_type=WIDE)


def low(v):
    return v.astype(NARROW)


def iota2(shape, dim):
    return lax.broadcasted_iota(jnp.int32, shape, dim)


def row_mean(v):
    return jnp.sum(v, axis=-1, keepdims=True) * (1.0 / v.shape[-1])


def norm_parts(v):
    center = v - row_mean(v)
    inv = lax.rsqrt(row_mean(center * center) + EPSILON)
    return center * inv, inv


def norm_back(xhat, inv, gain, up):
    u = up * gain
    return (u - row_mean(u) - xhat * row_mean(u * xhat)) * inv


def owners():
    out = []
    for dp in range(8):
        for slot in range(4):
            z, x, y, c = dp // 2, dp % 2, slot // 2, slot % 2
            a, b = (y, x) if c == 0 else (x, y)
            out.append((dp * 4 + slot, c, a * 8 + b * 4 + z, dp, slot))
    return out


def block_kernel(linked, n_in, n_out, *refs):
    ins, outs, scr = refs[:n_in], refs[n_in : n_in + n_out], refs[n_in + n_out :]
    inputs_ref, starts_ref, cot_ref = ins[:3]
    out_ref, gin_ref = outs[:2]
    (x_v, cot_v, w_first, w_out_v, w_up_v, w_down_v, perm, gains, n1, n1t, proj, expo, score, prob,
     rtot, scaled, att, middle, n2, n2t, gf, gft, acc, gtwo, ga, gproj, gnum, gtot, outb, gone,
     vis, vist, hcar, tail, passf, hcar_n, tail_n, loc, sin, tloc, tin, bd_lo, bd_hi, bdm, xsend, xrecv, tsend, trecv,
     ssem, rsem, lsem) = scr[:51]
    rest = scr[51:]

    slot = lax.axis_index("slot")
    dp = lax.axis_index("dp")
    y, c = slot // 2, slot % 2
    row, half = y, c
    tokens = x_v.shape[0]
    chunks = tokens // CHUNK
    partner = (dp, y * 2 + (1 - c))
    y_peer = (dp, (1 - y) * 2 + c)
    if linked:
        ag1, ag2, rs1, rs2, rc1, rc2, ra1, ra2, rb1, rb2, rz1, rz2 = rest
        z, x = dp // 2, dp % 2
        xa = y + c * (x - y)
        xb = x + c * (y - x)
        place = xa * 8 + xb * 4 + z
        dev_a = ((z * 2 + x + c * (1 - 2 * x)), slot + (1 - c) * 2 * (1 - 2 * y))
        dev_b = ((z * 2 + x + (1 - c) * (1 - 2 * x)), slot + c * 2 * (1 - 2 * y))
        peers = [partner, dev_a, dev_b] + [((((z + s) % 4) * 2 + x), slot) for s in (1, 2, 3)]
    else:
        peers = [partner, y_peer]

    barrier = pltpu.get_barrier_semaphore()
    for peer in peers:
        pl.semaphore_signal(barrier, inc=1, device_id=peer, device_id_type=MESH)

    own_rows = pl.ds(pl.multiple_of(half * tokens, tokens), tokens)
    x_copy = pltpu.make_async_copy(inputs_ref.at[row, own_rows], x_v, lsem.at[0])
    cot_copy = pltpu.make_async_copy(cot_ref.at[row, own_rows], cot_v, lsem.at[1])
    x_copy.start()
    cot_copy.start()

    def remote(src, dst, at, device):
        return pltpu.make_async_remote_copy(
            src_ref=src, dst_ref=dst, send_sem=ssem.at[at], recv_sem=rsem.at[at],
            device_id=device, device_id_type=MESH,
        )

    def gather_z(buf, at):
        return [
            remote(buf.at[c, place], buf.at[c, place], at + s - 1, ((((z + s) % 4) * 2 + x), slot))
            for s in (1, 2, 3)
        ]

    def gather_b(buf, at):
        part = buf.at[c, pl.ds(xa * 8 + xb * 4, 4)]
        return [remote(part, part, at + 3, dev_b), remote(part, part, at + 5, partner)]

    def gather_a(buf, at):
        part = buf.at[c, pl.ds(xa * 8, 8)]
        other = buf.at[c, pl.ds(xa * 8 + (1 - xb) * 4, 4)]
        return [remote(part, part, at + 4, dev_a), remote(other, other, at + 6, partner)]

    def gather_last(buf, at):
        part = buf.at[c, pl.ds((1 - xa) * 8, 8)]
        return [remote(part, part, at + 7, partner)]

    def start(copies):
        for copy in copies:
            copy.start()

    def recv(copies):
        for copy in copies:
            copy.wait_recv()

    def sent(copies):
        for copy in copies:
            copy.wait_send()

    def scatter_core(buf, got, at):
        return remote(buf.at[1 - c], got, at, partner)

    def scatter_a(buf, got, at):
        return remote(buf.at[c, pl.ds((1 - xa) * 8, 8)], got, at + 1, dev_a)

    def scatter_b(buf, got, at):
        return remote(buf.at[c, pl.ds(xa * 8 + (1 - xb) * 4, 4)], got, at + 2, dev_b)

    def scatter_z(buf, got, at):
        return [
            remote(
                buf.at[c, xa * 8 + xb * 4 + (z + s) % 4], got.at[s - 1], at + 2 + s,
                ((((z + s) % 4) * 2 + x), slot),
            )
            for s in (1, 2, 3)
        ]

    def add_blocks(buf, got, first, count):
        def step(i, _):
            at = first + i
            buf[c, at] = low(buf[c, at].astype(WIDE) + got[i].astype(WIDE))
            return 0

        lax.fori_loop(0, count, step, 0)

    LOCAL1, LOCAL2 = 0, 8
    STATE, BACK, OUT, GIN, SC2, SC1 = 16, 18, 20, 23, 26, 32

    ins_w = ins[3:]
    if linked:
        wq, wk, wv, wo, ws, wu, wd, ga1, ga2 = ins_w
        for n, shard in enumerate((wq, wk, wv)):
            for t in range(4):
                ag1[c, place, pl.ds(n * 64 + t * 16, 16), :] = shard[:, t * 128 : t * 128 + 128]
        ag1[c, place, pl.ds(192, 64), :] = ws[...]
        rows16 = iota2((16, 16), 0)
        both = jnp.where(
            rows16 == 0,
            jnp.broadcast_to(ga1[...].astype(WIDE), (16, 16)),
            jnp.where(rows16 == 1, jnp.broadcast_to(ga2[...].astype(WIDE), (16, 16)), 0.0),
        )
        lane_at = ((dp * 4 + slot) % 8) * 16
        spread = jnp.where(iota2((16, 128), 1) == iota2((16, 128), 0) + lane_at, 1.0, 0.0)
        ag1[c, place, pl.ds(256, 16), :] = low(dot(low(both), low(spread)))
        for t in range(4):
            ag2[c, place, pl.ds(t * 16, 16), :] = wo[:, t * 128 : t * 128 + 128]
            ag2[c, place, pl.ds(64 + t * 64, 64), :] = wu[:, t * 128 : t * 128 + 128]
        eye = low(jnp.where(iota2((64, 64), 0) == iota2((64, 64), 1), 1.0, 0.0))
        for t in range(4):
            ag2[c, place, pl.ds(320 + t * 64, 64), :] = low(dot_nt(eye, wd[t * 128 : t * 128 + 128, :]))
        pl.semaphore_wait(barrier, len(peers))
        start(gather_z(ag1, LOCAL1))
    else:
        fw_q, fw_k, fw_v, fw_o, fw_s, fw_u, fw_d, fg1, fg2 = ins_w
        pl.semaphore_wait(barrier, len(peers))
        copies = [
            pltpu.make_async_copy(src, dst, lsem.at[4 + i])
            for i, (src, dst) in enumerate((
                (fw_q, w_first.at[0]), (fw_k, w_first.at[1]), (fw_v, w_first.at[2]), (fw_s, w_first.at[3]),
                (fw_o, w_out_v), (fw_u, w_up_v), (fw_d, w_down_v),
            ))
        ]
        start(copies)
        for copy in copies:
            copy.wait()
        gains[0:1, :] = fg1[...].astype(WIDE)
        gains[1:2, :] = fg2[...].astype(WIDE)

    lane = iota2((CHUNK, LANES), 1)
    sub = iota2((CHUNK, LANES), 0)
    bd_lo[...] = low(jnp.where(lane < 64, 1.0, 0.0))
    bd_hi[...] = low(jnp.where(lane < 64, 0.0, 1.0))
    bdm[...] = jnp.where((lane < 64) == (sub < 64), 1.0, 0.0)
    upper = low(jnp.where(sub <= lane, 1.0, 0.0))
    lower = low(jnp.where(sub >= lane, 1.0, 0.0))
    ones = jnp.ones((CHUNK, LANES), NARROW)
    for n in range(chunks):
        begin = starts_ref[:, pl.ds(pl.multiple_of(half * tokens + n * CHUNK, CHUNK), CHUNK)].astype(WIDE)
        begin = jnp.where(row == 0, begin[0:1], begin[1:2])
        begin = low(jnp.broadcast_to(begin, (CHUNK, LANES)))
        by_lane = dot(begin, upper)
        by_row = dot_nt(lower, begin)
        total = dot(begin, ones)
        same = by_row == by_lane
        v = low(jnp.where(same & (sub >= lane), 1.0, 0.0))
        vt = low(jnp.where(same & (sub <= lane), 1.0, 0.0))
        vis[n, :, 0:128] = v
        vis[n, :, 128:256] = v
        vist[n, :, 0:128] = vt
        vist[n, :, 128:256] = vt
        carried = jnp.where(by_row == 0.0, 1.0, 0.0)
        ending = jnp.where(by_row == total, 1.0, 0.0)
        hcar[n] = carried
        tail[n] = ending
        hcar_n[n] = low(carried)
        tail_n[n] = low(ending)
        passf[n] = jnp.where(total == 0.0, 1.0, 0.0)

    def perm_rows(i, _):
        r = iota2((CHUNK, WIDTH), 0) + i * CHUNK
        n = iota2((CHUNK, WIDTH), 1)
        source = ((n >> 4) & 3) * 128 + (n & 15) * 8 + (n >> 6)
        perm[pl.ds(pl.multiple_of(i * CHUNK, CHUNK), CHUNK), :] = low(jnp.where(r == source, 1.0, 0.0))
        return 0

    lax.fori_loop(0, WIDTH // CHUNK, perm_rows, 0)
    x_copy.wait()

    if linked:
        zs = gather_z(ag1, LOCAL1)
        recv(zs)
        bs = gather_b(ag1, LOCAL1)
        start(bs)
        start(gather_z(ag2, LOCAL2))
        recv(bs[:1])
        as_ = gather_a(ag1, LOCAL1)
        start(as_)
        recv(as_[:1])
        ls = gather_last(ag1, LOCAL1)
        start(ls)
        recv(bs[1:])
        recv(as_[1:])
        recv(ls)
        for index, core, at, odp, oslot in owners():
            for n in range(3):
                for t in range(4):
                    w_first[n, index * 16 : index * 16 + 16, t * 128 : t * 128 + 128] = ag1[
                        core, at, n * 64 + t * 16 : n * 64 + t * 16 + 16, :
                    ]
            w_first[3, odp * 64 : odp * 64 + 64, oslot * 128 : oslot * 128 + 128] = ag1[core, at, 192:256, :]
        for window in range(4):
            total = jnp.zeros((16, 128), WIDE)
            for index, core, at, _, _ in owners():
                if index // 8 == window:
                    total = total + ag1[core, at, 256:272, :].astype(WIDE)
            gains[0:8, window * 128 : window * 128 + 128] = total[0:8]
    w_first[3] = low(dot(w_first[3], perm[...]))

    gain_one = gains[0:1, :]
    gain_two = gains[1:2, :]

    def by_chunk(body):
        def step(i, _):
            body(pl.ds(pl.multiple_of(i * CHUNK, CHUNK), CHUNK), i)
            return 0

        lax.fori_loop(0, chunks, step, 0)

    def norm_one(rows, i):
        xhat, _ = norm_parts(x_v[rows, :])
        n1[rows, :] = low(xhat * gain_one)

    by_chunk(norm_one)
    for n in range(3):
        proj[n] = low(dot(n1[...], w_first[n]))
    expo[...] = jnp.exp(dot(n1[...], w_first[3]))
    proj[3] = low(expo[...])
    n1t[...] = n1[...].T

    def two(v):
        return jnp.concatenate([v * bd_lo[...], v * bd_hi[...]], axis=0)

    def local_states(rows, i):
        w_tail = proj[3, rows, :]
        tloc[i] = jnp.broadcast_to(
            dot(jnp.ones((8, CHUNK), NARROW), w_tail * jnp.concatenate([tail_n[i]] * PAIRS, axis=1)),
            (8, WIDTH),
        )
        for p in range(PAIRS):
            cols = slice(p * 128, p * 128 + 128)
            w = proj[3, rows, cols]
            loc[0, i, p] = dot_tn(proj[1, rows, cols] * tail_n[i], w) * bdm[...]
            loc[1, i, p] = dot_tn(w * tail_n[i], proj[2, rows, cols]) * bdm[...]

    by_chunk(local_states)

    def scan_states(order, initial, t_initial, keep):
        def one(kind, p):
            state = initial(kind, p)
            for i in order:
                if keep:
                    sin[kind, i, p] = low(state)
                state = loc[kind, i, p] + passf[i] * state
            if not keep:
                xsend[kind, p] = state

        def step(k, _):
            one(k // PAIRS, k % PAIRS)
            return 0

        lax.fori_loop(0, 2 * PAIRS, step, 0)
        state = t_initial()
        for i in order:
            if keep:
                tin[i] = state
            state = tloc[i] + jnp.concatenate([passf[i, 0:8, :]] * PAIRS, axis=1) * state
        if not keep:
            tsend[...] = state

    def exchange(at):
        return [remote(xsend, xrecv.at[(at - STATE) // 2], at, partner), remote(tsend, trecv.at[(at - STATE) // 2], at + 1, partner)]

    def scan_and_carry(order, at, takes):
        n = (at - STATE) // 2
        scan_states(order, lambda k, p: jnp.zeros((128, 128), WIDE), lambda: jnp.zeros((8, WIDTH), WIDE), False)
        copies = exchange(at)
        start(copies)
        recv(copies)
        scan_states(order, lambda k, p: xrecv[n, k, p] * takes, lambda: trecv[n] * takes, True)

    forward = list(range(chunks))
    takes_forward = half.astype(WIDE)
    scan_and_carry(forward, STATE, takes_forward)

    if linked:
        zs2 = gather_z(ag2, LOCAL2)
        bs2 = gather_b(ag2, LOCAL2)
        as2 = gather_a(ag2, LOCAL2)
        ls2 = gather_last(ag2, LOCAL2)
        recv(zs2)
        start(bs2)

    first_half = iota2((CHUNK, LANES), 1) < 64

    def over_heads(lo_part, hi_part):
        return jnp.where(first_half, lo_part, hi_part)

    def head_max(v):
        return over_heads(
            jnp.max(jnp.where(first_half, v, -jnp.inf), axis=-1, keepdims=True),
            jnp.max(jnp.where(first_half, -jnp.inf, v), axis=-1, keepdims=True),
        )

    def head_sum(v):
        return over_heads(
            jnp.sum(jnp.where(first_half, v, 0.0), axis=-1, keepdims=True),
            jnp.sum(jnp.where(first_half, 0.0, v), axis=-1, keepdims=True),
        )

    def attend(rows, i):
        mask = vis[i]
        carried = hcar[i]
        totals = dot(mask[:, 0:128], proj[3, rows, :]) + jnp.concatenate([carried] * PAIRS, axis=1) * tin[i, 0:1, :]
        rtot[rows, :] = 1.0 / totals
        for p in range(PAIRS):
            cols = slice(p * 128, p * 128 + 128)
            q, k, v, w = (proj[n, rows, cols] for n in range(4))
            w2 = two(w)
            r = rtot[rows, cols]
            cross = low(dot_nt(q, two(k))) * mask
            s = (dot(cross, w2) + carried * dot(q, sin[0, i, p])) * r
            e = jnp.exp(s - head_max(s))
            pr = e / head_sum(e)
            sc = low(pr * r)
            mix = low(dot_nt(sc, w2)) * mask
            score[rows, cols] = s
            prob[rows, cols] = pr
            scaled[rows, cols] = sc
            att[rows, cols] = low(dot(mix, two(v)) + carried * dot(sc, sin[1, i, p]))

    by_chunk(attend)

    if linked:
        recv(bs2[:1])
        start(as2)
        recv(as2[:1])
        start(ls2)
        recv(bs2[1:])
        recv(as2[1:])
        recv(ls2)
        for index, core, at, odp, oslot in owners():
            for t in range(4):
                cols = slice(t * 128, t * 128 + 128)
                w_out_v[index * 16 : index * 16 + 16, cols] = ag2[core, at, t * 16 : t * 16 + 16, :]
                w_up_v[oslot, odp * 64 : odp * 64 + 64, cols] = ag2[core, at, 64 + t * 64 : 128 + t * 64, :]
                w_down_v[oslot, odp * 64 : odp * 64 + 64, cols] = ag2[core, at, 320 + t * 64 : 384 + t * 64, :]

    middle[...] = x_v[...] + dot(att[...], w_out_v[...])
    cot_copy.wait()

    def norm_two(rows, i):
        xhat, _ = norm_parts(middle[rows, :])
        n2[rows, :] = low(xhat * gain_two)
        gf[rows, :] = low(cot_v[rows, :])
        acc[rows, :] = jnp.zeros((CHUNK, WIDTH), WIDE)
        gtwo[rows, :] = jnp.zeros((CHUNK, WIDTH), WIDE)

    by_chunk(norm_two)
    n2t[...] = n2[...].T
    gft[...] = gf[...].T

    def feed(j, _):
        hidden = dot(n2[...], w_up_v[j])
        cdf = 0.5 * (1.0 + lax.erf(hidden * 0.7071067811865476))
        active = low(hidden * cdf)
        slope = cdf + hidden * (jnp.exp(-0.5 * hidden * hidden) * 0.3989422804014327)
        grad_hidden = low(dot(gf[...], w_down_v[j]) * slope)
        acc[...] += dot_nt(active, w_down_v[j])
        gtwo[...] += dot_nt(grad_hidden, w_up_v[j])
        g_up = low(dot(n2t[...], grad_hidden))
        g_down = low(dot(gft[...], active))
        if linked:
            jy, jc = j // 2, j % 2
            for odp in range(8):
                oz, ox = odp // 2, odp % 2
                at = (jy + jc * (ox - jy)) * 8 + (ox + jc * (jy - ox)) * 4 + oz
                for t in range(4):
                    rows, cols = slice(odp * 64, odp * 64 + 64), slice(t * 128, t * 128 + 128)
                    rs2[jc, at, pl.ds(64 + t * 64, 64), :] = g_up[rows, cols]
                    rs2[jc, at, pl.ds(320 + t * 64, 64), :] = g_down[rows, cols]
        else:
            outs[7][j] = g_up
            outs[8][j] = g_down
        return 0

    lax.fori_loop(0, 4, feed, 0)

    def spread_output(target, base):
        mine = target.at[row, own_rows]
        ycopy = remote(outb, mine, base, y_peer)
        ccopy = remote(outb, mine, base + 1, partner)
        lcopy = pltpu.make_async_copy(outb, mine, lsem.at[2 + (base - OUT) // 3])
        theirs = target.at[1 - row, own_rows]
        forward_copy = remote(theirs, theirs, base + 2, partner)
        return ycopy, ccopy, lcopy, forward_copy

    def norm_two_back(rows, i):
        outb[rows, :] = low(middle[rows, :] + acc[rows, :])
        xhat, inv = norm_parts(middle[rows, :])
        up = gtwo[rows, :]
        grad = cot_v[rows, :] + norm_back(xhat, inv, gain_two, up)
        cot_v[rows, :] = grad
        gf[rows, :] = low(grad)
        gains[3:4, :] = gains[3:4, :] + jnp.sum(up * xhat, axis=0, keepdims=True)

    gains[2:8, :] = jnp.zeros((6, WIDTH), WIDE)
    by_chunk(norm_two_back)
    oy, oc, ol, of = spread_output(out_ref, OUT)
    oy.start()
    oc.start()
    ol.start()
    ga[...] = low(dot_nt(gf[...], w_out_v[...]))
    g_out = low(dot_tn(att[...], gf[...]))
    if linked:
        for index, core, at, _, _ in owners():
            for t in range(4):
                rs2[core, at, t * 16 : t * 16 + 16, :] = g_out[index * 16 : index * 16 + 16, t * 128 : t * 128 + 128]
        c2 = scatter_core(rs2, rc2, SC2)
        c2.start()
    else:
        outs[5][...] = g_out

    def back_first(rows, i):
        mask = vis[i]
        carried = hcar[i]
        carried_n = hcar_n[i]
        for p in range(PAIRS):
            cols = slice(p * 128, p * 128 + 128)
            q, k, v, w = (proj[n, rows, cols] for n in range(4))
            w2 = two(w)
            g = ga[rows, cols]
            r, pr, s = rtot[rows, cols], prob[rows, cols], score[rows, cols]
            gmix = low(dot_nt(g, two(v))) * mask
            gs = low(dot(gmix, w2) + carried * dot_nt(g, sin[1, i, p])).astype(WIDE)
            gp = gs * r
            gscore = pr * (gp - head_sum(pr * gp))
            gt = low(-(gs * pr * r + gscore * s) * r)
            gn = low(gscore * r)
            gcross = low(dot_nt(gn, w2)) * mask
            gproj[0, rows, cols] = low(dot(gcross, two(k)) + carried * dot_nt(gn, sin[0, i, p]))
            gnum[rows, cols] = gn
            gtot[rows, cols] = gt
            loc[0, i, p] = dot_tn(q * carried_n, gn) * bdm[...]
            loc[1, i, p] = dot_tn(g * carried_n, scaled[rows, cols]) * bdm[...]
        tloc[i] = jnp.broadcast_to(
            dot(jnp.ones((8, CHUNK), NARROW), gtot[rows, :] * jnp.concatenate([carried_n] * PAIRS, axis=1)),
            (8, WIDTH),
        )

    by_chunk(back_first)
    if linked:
        c2.wait_recv()
        add_blocks(rs2, rc2, 0, 16)
        a2 = scatter_a(rs2, ra2, SC2)
        a2.start()
    oy.wait_recv()
    of.start()
    sent(exchange(STATE))
    scan_and_carry(forward[::-1], BACK, 1.0 - takes_forward)

    def back_second(rows, i):
        mask = vist[i]
        ends = tail[i]
        wc = dot(mask[:, 0:128], gtot[rows, :]) + jnp.concatenate([ends] * PAIRS, axis=1) * tin[i, 0:1, :]
        for p in range(PAIRS):
            cols = slice(p * 128, p * 128 + 128)
            q, k, v, w = (proj[n, rows, cols] for n in range(4))
            g, sc, gn = ga[rows, cols], scaled[rows, cols], gnum[rows, cols]
            g2, sc2, gn2, q2 = two(g), two(sc), two(gn), two(q)
            s_query, s_grad = sin[0, i, p], sin[1, i, p]
            gmix = low(dot_nt(v, g2)) * mask
            mix = low(dot_nt(w, sc2)) * mask
            gcross = low(dot_nt(w, gn2)) * mask
            cross = low(dot_nt(k, q2)) * mask
            gw = dot(gmix, sc2) + dot(cross, gn2) + ends * (dot(v, s_grad) + dot(k, s_query)) + wc[:, cols]
            gproj[3, rows, cols] = low(low(gw).astype(WIDE) * expo[rows, cols])
            gproj[2, rows, cols] = low(dot(mix, g2) + ends * dot_nt(w, s_grad))
            gproj[1, rows, cols] = low(dot(gcross, q2) + ends * dot_nt(w, s_query))

    by_chunk(back_second)

    gone[...] = dot_nt(gproj[0], w_first[0])
    for n in range(1, 4):
        gone[...] += dot_nt(gproj[n], w_first[n])
    ol.wait()
    oy.wait_send()
    oc.wait_send()

    def norm_one_back(rows, i):
        xhat, inv = norm_parts(x_v[rows, :])
        up = gone[rows, :]
        outb[rows, :] = low(cot_v[rows, :] + norm_back(xhat, inv, gain_one, up))
        gains[2:3, :] = gains[2:3, :] + jnp.sum(up * xhat, axis=0, keepdims=True)

    by_chunk(norm_one_back)
    iy, ic, il, if_ = spread_output(gin_ref, GIN)
    iy.start()
    ic.start()
    il.start()

    for n in range(4):
        grad = low(dot(n1t[...], gproj[n]))
        if n == 3:
            grad = low(dot_nt(grad, perm[...]))
        if not linked:
            outs[(2, 3, 4, 6)[n]][...] = grad
            continue
        for index, core, at, odp, oslot in owners():
            if n == 3:
                rs1[core, at, 192:256, :] = grad[odp * 64 : odp * 64 + 64, oslot * 128 : oslot * 128 + 128]
            else:
                for t in range(4):
                    rs1[core, at, n * 64 + t * 16 : n * 64 + t * 16 + 16, :] = grad[
                        index * 16 : index * 16 + 16, t * 128 : t * 128 + 128
                    ]
    if linked:
        for index, core, at, _, _ in owners():
            window = index // 8
            rs1[core, at, 256:272, :] = low(
                jnp.concatenate(
                    [gains[2:4, window * 128 : window * 128 + 128], jnp.zeros((14, 128), WIDE)], axis=0
                )
            )
        c1 = scatter_core(rs1, rc1, SC1)
        c1.start()
        a2.wait_recv()
        add_blocks(rs2, ra2, xa * 8, 8)
        b2 = scatter_b(rs2, rb2, SC2)
        b2.start()
        c1.wait_recv()
        add_blocks(rs1, rc1, 0, 16)
        a1 = scatter_a(rs1, ra1, SC1)
        a1.start()
        b2.wait_recv()
        add_blocks(rs2, rb2, xa * 8 + xb * 4, 4)
        z2 = scatter_z(rs2, rz2, SC2)
        start(z2)
        a1.wait_recv()
        add_blocks(rs1, ra1, xa * 8, 8)
        b1 = scatter_b(rs1, rb1, SC1)
        b1.start()
        b1.wait_recv()
        add_blocks(rs1, rb1, xa * 8 + xb * 4, 4)
        z1 = scatter_z(rs1, rz1, SC1)
        start(z1)
        iy.wait_recv()
        if_.start()
        recv(z2)

        def summed(buf, got, first, count):
            rows = pl.ds(first, count)
            total = buf[c, place, rows, :].astype(WIDE)
            for s in range(3):
                total = total + got[s, rows, :].astype(WIDE)
            return total

        oq, ok, ov, oo, os_, ou, od, og = outs[2:]
        for t in range(4):
            cols = slice(t * 128, t * 128 + 128)
            oo[:, cols] = summed(rs2, rz2, t * 16, 16)
            ou[:, cols] = summed(rs2, rz2, 64 + t * 64, 64)
            od[:, cols] = summed(rs2, rz2, 320 + t * 64, 64)
        recv(z1)
        for n, target in enumerate((oq, ok, ov)):
            for t in range(4):
                target[:, t * 128 : t * 128 + 128] = summed(rs1, rz1, n * 64 + t * 16, 16)
        os_[...] = summed(rs1, rz1, 192, 64)
        og[...] = summed(rs1, rz1, 256, 16)
    else:
        outs[9][...] = gains[2:4, :]
        iy.wait_recv()
        if_.start()

    oc.wait_recv()
    of.wait()
    il.wait()
    iy.wait_send()
    ic.wait()
    if_.wait()
    sent(exchange(BACK))
    if linked:
        for buf, at in ((ag1, LOCAL1), (ag2, LOCAL2)):
            sent(gather_z(buf, at) + gather_b(buf, at) + gather_a(buf, at) + gather_last(buf, at))
        sent([c1, c2, a1, a2, b1, b2] + z1 + z2)


def run_block(linked, inputs, starts, cotangent, weights):
    rows, length, width = inputs.shape
    tokens = length // 2
    chunks = tokens // CHUNK
    vm = pltpu.VMEM
    scratch = [
        vm((tokens, width), WIDE), vm((tokens, width), WIDE),
        vm((4, width, width), NARROW), vm((width, width), NARROW),
        vm((4, width, width), NARROW), vm((4, width, width), NARROW),
        vm((width, width), NARROW), vm((8, width), WIDE),
        vm((tokens, width), NARROW), vm((width, tokens), NARROW),
        vm((4, tokens, width), NARROW), vm((tokens, width), WIDE),
        vm((tokens, width), WIDE), vm((tokens, width), WIDE), vm((tokens, width), WIDE),
        vm((tokens, width), NARROW), vm((tokens, width), NARROW),
        vm((tokens, width), WIDE), vm((tokens, width), NARROW), vm((width, tokens), NARROW),
        vm((tokens, width), NARROW), vm((width, tokens), NARROW),
        vm((tokens, width), WIDE), vm((tokens, width), WIDE),
        vm((tokens, width), NARROW), vm((4, tokens, width), NARROW),
        vm((tokens, width), NARROW), vm((tokens, width), NARROW),
        vm((tokens, width), NARROW), vm((tokens, width), WIDE),
        vm((chunks, CHUNK, 256), NARROW), vm((chunks, CHUNK, 256), NARROW),
        vm((chunks, CHUNK, LANES), WIDE), vm((chunks, CHUNK, LANES), WIDE), vm((chunks, CHUNK, LANES), WIDE),
        vm((chunks, CHUNK, LANES), NARROW), vm((chunks, CHUNK, LANES), NARROW),
        vm((2, chunks, PAIRS, 128, 128), WIDE), vm((2, chunks, PAIRS, 128, 128), NARROW),
        vm((chunks, 8, width), WIDE), vm((chunks, 8, width), WIDE),
        vm((CHUNK, LANES), NARROW), vm((CHUNK, LANES), NARROW), vm((CHUNK, LANES), WIDE),
        vm((2, PAIRS, 128, 128), WIDE), vm((2, 2, PAIRS, 128, 128), WIDE),
        vm((8, width), WIDE), vm((2, 8, width), WIDE),
        pltpu.SemaphoreType.DMA((40,)), pltpu.SemaphoreType.DMA((40,)), pltpu.SemaphoreType.DMA((12,)),
    ]
    if linked:
        scratch += [
            vm((2, 16, EARLY, LANES), NARROW), vm((2, 16, LATE, LANES), NARROW),
            vm((2, 16, EARLY, LANES), NARROW), vm((2, 16, LATE, LANES), NARROW),
            vm((16, EARLY, LANES), NARROW), vm((16, LATE, LANES), NARROW),
            vm((8, EARLY, LANES), NARROW), vm((8, LATE, LANES), NARROW),
            vm((4, EARLY, LANES), NARROW), vm((4, LATE, LANES), NARROW),
            vm((3, EARLY, LANES), NARROW), vm((3, LATE, LANES), NARROW),
        ]
    anywhere = pl.BlockSpec(memory_space=pl.ANY)
    here = pl.BlockSpec(memory_space=pltpu.VMEM)
    shape = jax.ShapeDtypeStruct
    big = [shape((rows, length, width), NARROW)] * 2
    square = (width, width)
    if linked:
        small = [shape((16, width), WIDE)] * 4 + [
            shape((64, 128), WIDE), shape((64, width), WIDE), shape((64, width), WIDE), shape((16, 128), WIDE)
        ]
        weight_specs = [here] * 9
    else:
        small = [shape(square, NARROW)] * 5 + [shape((4, *square), NARROW)] * 2 + [shape((2, width), WIDE)]
        weight_specs = [anywhere] * 7 + [here] * 2
    return pl.pallas_call(
        functools.partial(block_kernel, linked, 12, 2 + len(small)),
        out_shape=big + small,
        in_specs=[anywhere, here, anywhere] + weight_specs,
        out_specs=[anywhere] * 2 + [here] * len(small),
        scratch_shapes=scratch,
        compiler_params=pltpu.CompilerParams(
            collective_id=0, has_side_effects=True, vmem_limit_bytes=62 * 1024 * 1024
        ),
    )(inputs, starts, cotangent, *weights)


def on_device(
    inputs, starts, w_query, w_key, w_value, w_out, w_slot, w_up, w_down, gain_attn, gain_ffn, cotangent
):
    n_dp, n_slot = lax.axis_size("dp"), lax.axis_size("slot")
    if n_dp == 8 and n_slot == 4:
        weights = (
            w_query, w_key, w_value, w_out, w_slot, w_up, w_down,
            gain_attn.reshape(1, -1), gain_ffn.reshape(1, -1),
        )
        out, gin, gq, gk, gv, go, gs, gu, gd, gg = run_block(True, inputs, starts, cotangent, weights)
        at = ((lax.axis_index("dp") * n_slot + lax.axis_index("slot")) % 8) * 16
        gains = lax.dynamic_slice(gg, (0, at), (2, 16))
        return (
            out.astype(WIDE), gin.astype(WIDE), gq, gk, gv, go, gs, gu, gd.T, gains[0], gains[1],
        )

    def whole(v, names, axis):
        return lax.all_gather(v, names, axis=axis, tiled=True)

    both = ("dp", "slot")
    width = inputs.shape[-1]
    up = whole(whole(w_up, "dp", 0), "slot", 1).reshape(width, n_slot, -1).transpose(1, 0, 2)
    down = whole(whole(w_down, "dp", 1), "slot", 0).reshape(n_slot, -1, width).transpose(0, 2, 1)
    weights = (
        whole(w_query, both, 0), whole(w_key, both, 0), whole(w_value, both, 0), whole(w_out, both, 0),
        whole(whole(w_slot, "dp", 0), "slot", 1), up, down,
        whole(gain_attn, both, 0).reshape(1, -1), whole(gain_ffn, both, 0).reshape(1, -1),
    )
    out, gin, gq, gk, gv, go, gs, gu, gd, gg = run_block(False, inputs, starts, cotangent, weights)

    def shared(v, names, axis):
        return lax.psum_scatter(v.astype(WIDE), names, scatter_dimension=axis, tiled=True)

    gu = gu.transpose(1, 0, 2).reshape(width, -1)
    gd = gd.transpose(0, 2, 1).reshape(-1, width)
    return (
        out.astype(WIDE), gin.astype(WIDE),
        shared(gq, both, 0), shared(gk, both, 0), shared(gv, both, 0), shared(go, both, 0),
        shared(shared(gs, "slot", 1), "dp", 0), shared(shared(gu, "slot", 1), "dp", 0),
        shared(shared(gd, "slot", 0), "dp", 1), shared(gg[0], both, 0), shared(gg[1], both, 0),
    )


def solution(mesh):
    every = ("dp", "slot")
    rows = P("dp", None, None)
    return jax.shard_map(
        on_device,
        mesh=mesh,
        in_specs=(
            rows, P("dp", None), P(every, None), P(every, None), P(every, None), P(every, None),
            P("dp", "slot"), P("dp", "slot"), P("slot", "dp"), P(every), P(every), rows,
        ),
        out_specs=(
            rows, rows, P(every, None), P(every, None), P(every, None), P(every, None),
            P("dp", "slot"), P("dp", "slot"), P("slot", "dp"), P(every), P(every),
        ),
        check_vma=False,
    )
```

time: 1970 us -> 150 us (0.08)
  blocking collectives: 723 us -> 0 us
  waiting for transfers between devices: 649 us -> 0 us
  matrix products: 386 us -> 0 us
  Pallas kernels: 0 us -> 135 us
  local copies, waits for them, and re-layouts: 127 us -> 7.43 us
  other arithmetic: 59.4 us -> 6.81 us
    reduce_scatter x7 -> x0, waiting for transfers between devices: 547 us -> none  [the longest x1 137 us: on_device(): lax.psum_scatter(grad_out_w, ('dp', 'slot'), scatter_dimension=0, tiled=T...]
    dot_general x103 -> x0, matrix products: 386 us -> none  [the longest x96 366 us: einsum_wide(): return jnp.einsum(pattern, first_op, second_op, preferred_element_type=WIDE)]
    psum x2 -> x0, blocking collectives: 383 us -> none  [the longest x1 307 us: on_device(): lax.psum((grad_heads[0], grad_heads[1], grad_heads[2], grad_heads[3]), 's...]
    all_gather x7 -> x0, blocking collectives: 258 us -> none  [the longest x1 41.6 us: on_device(): lax.all_gather(w_query, ('dp', 'slot'), axis=0, tiled=True)]
    pallas_call x0 -> x1, Pallas kernels: none -> 135 us  [run_block(): pl.pallas_call(functools.partial(block_kernel, linked, 12, 2 + len(small)...]
    psum x4 -> x0, waiting for transfers between devices: 102 us -> none  [the longest x1 74.6 us: on_device(): grad_second = lax.psum(grad_part, 'slot')]
    unnamed x2 -> x0, blocking collectives: 81.7 us -> none
    unnamed x122 -> x24, local copies, waits for them, and re-layouts: 43.9 us -> 6.02 us
  transfers between devices with their start and end apart: 12 -> 0, of which waited for: 7 -> 0; matrix products, arithmetic and copies ran while one was open for 6% -> 0% of each run, Pallas kernels for 0% -> 0%
where the time goes in v1:
time: 150 us
  Pallas kernels  135 us (90%)
  local copies, waits for them, and re-layouts  7.43 us (5%)
  other arithmetic  6.81 us (5%)
    pallas_call x1, Pallas kernels, run_block(): pl.pallas_call(functools.partial(block_kernel, linked, 12, 2 + len(small)...  135 us
    unnamed x24, local copies, waits for them, and re-layouts  6.02 us
    convert_element_type x1, other arithmetic, on_device(): out.astype(WIDE)  4.2 us

profile of v1, /device:TPU:0, one launch (start us, length us, event | category | flops | bytes accessed | tf_op | source)
XLA Modules:
  0.0 149.7 jit_solution(10126676883330496062)
XLA Ops:
  0.7 1.6 %copy.23.refs_9_ = bf16[512,64]{1,0:T(8,128)(2,1)} copy(bf16[512,64]{0,1:T(8,128)(2,1)} %param.20) | data formatting | bytes 131072 | tf_op args[8]
  2.3 134.7 %shard_map.203 = (bf16[2,1024,512]{2,1,0:T(8,128)(2,1)}, bf16[2,1024,512]{2,1,0:T(8,128)(2,1)}, f32[16,512]{1,0:T(8,128)}, f32[16,512]{1,0:T(8,128)}, f32[16,512...) custom-call(f32[2,1024,512]{2,1,0:T(8,128)} %refs_0_.1, ...), custom_call_target="tpu_custom_call" | custom-call | tf_op jit(solution)/shard_map/pallas_call | solution.py:715
  137.0 0.0 copy-start
  137.0 0.9 constant_dynamic-slice_fusion
  137.9 0.5 slice_bitcast_fusion
  138.4 4.2 %convert_element_type.6 = f32[2,1024,512]{2,1,0:T(8,128)} convert(bf16[2,1024,512]{2,1,0:T(8,128)(2,1)} %get-tuple-element.21) | non-fusion elementwise | flops 1048576 | bytes 6291456 | tf_op jit(solution)/shard_map/convert_element_type | solution.py:740
  142.6 0.0 copy-done
  142.6 0.0 copy-start.7
  142.6 0.0 copy-start.6
  142.6 0.0 copy-start.5
  142.6 0.0 copy-start.4
  142.7 0.0 copy-start.3
  142.7 0.0 copy-start.2
  142.7 0.0 copy-start.1
  142.7 2.6 %convert_element_type.7 = f32[2,1024,512]{2,1,0:T(8,128)} convert(bf16[2,1024,512]{2,1,0:T(8,128)(2,1)S(1)} %copy-done) | non-fusion elementwise | flops 1048576 | bytes 6291456 | tf_op jit(solution)/shard_map/convert_element_type | solution.py:740
  145.3 0.0 copy-done.7
  145.3 0.6 copy.31
  145.9 0.0 copy-done.6
  145.9 0.6 copy.32
  146.5 0.0 copy-done.5
  146.5 0.6 copy.33
  147.1 0.0 copy-done.4
  147.1 0.6 copy.34
  147.8 0.0 copy-done.3
  147.8 0.6 copy.35
  148.4 0.0 copy-done.2
  148.4 0.7 copy.36
  149.0 0.0 copy-done.1
  149.0 0.7 copy.37
Async XLA Ops:
  137.0 5.6 %copy-start = (bf16[2,1024,512]{2,1,0:T(8,128)(2,1)S(1)}, bf16[2,1024,512]{2,1,0:T(8,128)(2,1)}, u32[]{:S(2)}) copy-start(bf16[2,1024,512]{2,1,0:T(8,128)(2,1)} %get-tuple-element.22) | copy-start | bytes 6291460
  142.6 2.7 %copy-start.7 = (f32[16,512]{1,0:T(8,128)S(1)}, f32[16,512]{1,0:T(8,128)}, u32[]{:S(2)}) copy-start(f32[16,512]{1,0:T(8,128)} %get-tuple-element.46) | copy-start | bytes 98308
  142.6 3.3 %copy-start.6 = (f32[16,512]{1,0:T(8,128)S(1)}, f32[16,512]{1,0:T(8,128)}, u32[]{:S(2)}) copy-start(f32[16,512]{1,0:T(8,128)} %get-tuple-element.47) | copy-start | bytes 98308
  142.6 3.9 %copy-start.5 = (f32[16,512]{1,0:T(8,128)S(1)}, f32[16,512]{1,0:T(8,128)}, u32[]{:S(2)}) copy-start(f32[16,512]{1,0:T(8,128)} %get-tuple-element.48) | copy-start | bytes 98308
  142.6 4.5 %copy-start.4 = (f32[16,512]{1,0:T(8,128)S(1)}, f32[16,512]{1,0:T(8,128)}, u32[]{:S(2)}) copy-start(f32[16,512]{1,0:T(8,128)} %get-tuple-element.49) | copy-start | bytes 98308
  142.7 5.1 %copy-start.3 = (f32[64,128]{1,0:T(8,128)S(1)}, f32[64,128]{1,0:T(8,128)}, u32[]{:S(2)}) copy-start(f32[64,128]{1,0:T(8,128)} %get-tuple-element.50) | copy-start | bytes 98308
  142.7 5.7 %copy-start.2 = (f32[64,512]{1,0:T(8,128)S(1)}, f32[64,512]{1,0:T(8,128)}, u32[]{:S(2)}) copy-start(f32[64,512]{1,0:T(8,128)} %get-tuple-element.51) | copy-start | bytes 393220
  142.7 6.4 %copy-start.1 = (f32[64,512]{1,0:T(8,128)S(1)}, f32[64,512]{1,0:T(8,128)}, u32[]{:S(2)}) copy-start(f32[64,512]{1,0:T(8,128)} %get-tuple-element.29) | copy-start | bytes 393220

commit v2 on v1

v2 whole, which is shorter than its diff:
```python
import functools

import jax
import jax.numpy as jnp
from jax import lax
from jax.experimental import pallas as pl
from jax.experimental.pallas import tpu as pltpu
from jax.sharding import PartitionSpec as P

HEADS = 8
EPSILON = 1e-05
NARROW = jnp.bfloat16
WIDE = jnp.float32
MESH = pl.DeviceIdType.MESH

WIDTH = 512
CHUNK = 128
PAIRS = 4
LANES = 128
PIECE_ROWS = (80, 64, 64, 64, 64, 128, 128, 128, 128)
SLOT, KEY, VALUE, QUERY, OUT_W, TILE = range(6)
SMALL_ROWS = sum(PIECE_ROWS)
GATHER_SEMS, SCATTER_SEMS = 8, 6


def dot(a, b):
    return lax.dot_general(a, b, (((1,), (0,)), ((), ())), preferred_element_type=WIDE)


def dot_nt(a, b):
    return lax.dot_general(a, b, (((1,), (1,)), ((), ())), preferred_element_type=WIDE)


def dot_tn(a, b):
    return lax.dot_general(a, b, (((0,), (0,)), ((), ())), preferred_element_type=WIDE)


def low(v):
    return v.astype(NARROW)


def iota2(shape, dim):
    return lax.broadcasted_iota(jnp.int32, shape, dim)


def row_mean(v):
    return jnp.sum(v, axis=-1, keepdims=True) * (1.0 / v.shape[-1])


def norm_parts(v):
    center = v - row_mean(v)
    inv = lax.rsqrt(row_mean(center * center) + EPSILON)
    return center * inv, inv


def norm_back(xhat, inv, gain, up):
    u = up * gain
    return (u - row_mean(u) - xhat * row_mean(u * xhat)) * inv


def owners(mixed):
    out = []
    for dp in range(8):
        for slot in range(4):
            z, x, y, c = dp // 2, dp % 2, slot // 2, slot % 2
            a, b = (y, x) if c == 0 and mixed else (x, y)
            out.append((dp * 4 + slot, c, a * 8 + b * 4 + z, dp, slot))
    return out


def square_of(buf):
    return jnp.concatenate(
        [
            jnp.concatenate([buf[core, at, t * 16 : t * 16 + 16, :] for t in range(4)], axis=1)
            for _, core, at, _, _ in owners(True)
        ],
        axis=0,
    )


def tile_of(buf, n, first):
    place = {(dp, slot): (core, at) for _, core, at, dp, slot in owners(True)}
    return jnp.concatenate(
        [
            jnp.concatenate(
                [buf[(n, *place[dp, slot], slice(first, first + 64), slice(None))] for dp in range(8)], axis=0
            )
            for slot in range(4)
        ],
        axis=1,
    )


def block_kernel(linked, n_in, n_out, *refs):
    ins, outs, scr = refs[:n_in], refs[n_in : n_in + n_out], refs[n_in + n_out :]
    inputs_ref, starts_ref, cot_ref = ins[:3]
    out_ref, gin_ref = outs[:2]
    (x_v, cot_v, w_slot, perm, gains, n1, n1t, proj, expo, score, prob,
     rtot, scaled, att, mid, acc, n2, n2t, gf, gft, gtwo, ga, gproj, gnum, gtot, outb, ginb,
     vis, vist, hcar, tail, passf, hcar_n, tail_n, loc, sin, tloc, tin, bd_lo, bd_hi, bdm, xsend, xrecv, tsend, trecv,
     ssem, rsem, lsem) = scr[:48]
    rest = scr[48:]

    slot = lax.axis_index("slot")
    dp = lax.axis_index("dp")
    y, c = slot // 2, slot % 2
    row, half = y, c
    tokens = x_v.shape[0]
    chunks = tokens // CHUNK
    partner = (dp, y * 2 + (1 - c))
    y_peer = (dp, (1 - y) * 2 + c)
    if linked:
        ags, rss, rcs, ras, rbs, rzs = (rest[6 * n : 6 * n + 6] for n in range(6))
        z, x = dp // 2, dp % 2
        xa = y + c * (x - y)
        xb = x + c * (y - x)
        place = xa * 8 + xb * 4 + z
        own = x * 8 + y * 4 + z
        x_peer = (z * 2 + 1 - x, slot)
        dev_a = ((z * 2 + x + c * (1 - 2 * x)), slot + (1 - c) * 2 * (1 - 2 * y))
        dev_b = ((z * 2 + x + (1 - c) * (1 - 2 * x)), slot + c * 2 * (1 - 2 * y))
        z_peers = [((((z + s) % 4) * 2 + x), slot) for s in (1, 2, 3)]
        peers = [partner, x_peer, y_peer] + z_peers
    else:
        peers = [partner, y_peer]

    barrier = pltpu.get_barrier_semaphore()
    for peer in peers:
        pl.semaphore_signal(barrier, inc=1, device_id=peer, device_id_type=MESH)

    own_rows = pl.ds(pl.multiple_of(half * tokens, tokens), tokens)
    x_copy = pltpu.make_async_copy(inputs_ref.at[row, own_rows], x_v, lsem.at[0])
    cot_copy = pltpu.make_async_copy(cot_ref.at[row, own_rows], cot_v, lsem.at[1])
    x_copy.start()
    cot_copy.start()

    def remote(src, dst, at, device):
        return pltpu.make_async_remote_copy(
            src_ref=src, dst_ref=dst, send_sem=ssem.at[at], recv_sem=rsem.at[at],
            device_id=device, device_id_type=MESH,
        )

    def start(copies):
        for copy in copies:
            copy.start()

    def recv(copies):
        for copy in copies:
            copy.wait_recv()

    def sent(copies):
        for copy in copies:
            copy.wait_send()

    def view(bufs, n):
        return bufs[n] if isinstance(n, int) and n < TILE else bufs[TILE].at[n - TILE]

    def gather_z(n):
        mine, at = view(ags, n).at[c, place], n * GATHER_SEMS
        return [remote(mine, mine, at + s, z_peers[s]) for s in range(3)]

    def gather_b(n):
        part, at = view(ags, n).at[c, pl.ds(xa * 8 + xb * 4, 4)], n * GATHER_SEMS
        return [remote(part, part, at + 3, dev_b), remote(part, part, at + 5, partner)]

    def gather_a(n):
        buf, at = view(ags, n), n * GATHER_SEMS
        part = buf.at[c, pl.ds(xa * 8, 8)]
        other = buf.at[c, pl.ds(xa * 8 + (1 - xb) * 4, 4)]
        return [remote(part, part, at + 4, dev_a), remote(other, other, at + 6, partner)]

    def gather_last(n):
        part = view(ags, n).at[c, pl.ds((1 - xa) * 8, 8)]
        return [remote(part, part, n * GATHER_SEMS + 7, partner)]

    def gather_step(n, stage):
        if stage == 0:
            start(gather_z(n))
        elif stage == 1:
            recv(gather_z(n))
            start(gather_b(n))
        elif stage == 2:
            recv(gather_b(n)[:1])
            start(gather_a(n))
        elif stage == 3:
            recv(gather_a(n)[:1])
            start(gather_last(n))
        else:
            recv(gather_b(n)[1:] + gather_a(n)[1:] + gather_last(n))

    def scatter_copies(n, stage):
        buf, at = view(rss, n), SCATTER + n * SCATTER_SEMS
        if stage == 0:
            return [remote(buf.at[1 - c], view(rcs, n), at, partner)]
        if stage == 1:
            return [remote(buf.at[c, pl.ds((1 - x) * 8, 8)], view(ras, n), at + 1, x_peer)]
        if stage == 2:
            return [remote(buf.at[c, pl.ds(x * 8 + (1 - y) * 4, 4)], view(rbs, n), at + 2, y_peer)]
        got = view(rzs, n)
        return [
            remote(buf.at[c, x * 8 + y * 4 + (z + s + 1) % 4], got.at[s], at + 3 + s, z_peers[s])
            for s in range(3)
        ]

    def scatter_step(n, stage, rows):
        if stage:
            recv(scatter_copies(n, stage - 1))
            buf = view(rss, n)
            if stage < 4:
                got = view((rcs, ras, rbs)[stage - 1], n)
                first, count = ((0, 16), (x * 8, 8), (x * 8 + y * 4, 4))[stage - 1]

                def step(i, _):
                    at = first + i
                    buf[c, at] = low(buf[c, at].astype(WIDE) + got[i].astype(WIDE))
                    return 0

                lax.fori_loop(0, count, step, 0)
            else:
                got = view(rzs, n)
                total = buf[c, own].astype(WIDE)
                for s in range(3):
                    total = total + got[s].astype(WIDE)
                base = sum(PIECE_ROWS[:n]) if isinstance(n, int) else sum(PIECE_ROWS[:TILE]) + (n - TILE) * 128
                small_ref[pl.ds(base, rows), :] = total
        if stage < 4:
            start(scatter_copies(n, stage))

    SCATTER = 9 * GATHER_SEMS
    STATE = SCATTER + 9 * SCATTER_SEMS
    BACK, OUT, GIN = STATE + 2, STATE + 4, STATE + 7

    ins_w = ins[3:]
    if linked:
        small_ref = outs[2]
        wq, wk, wv, wo, ws, wu, wd, ga1, ga2 = ins_w
        for n, shard in ((QUERY, wq), (KEY, wk), (VALUE, wv), (OUT_W, wo)):
            for t in range(4):
                ags[n][c, place, pl.ds(t * 16, 16), :] = shard[:, t * 128 : t * 128 + 128]
        ags[SLOT][c, place, pl.ds(0, 64), :] = ws[...]
        rows16 = iota2((16, 16), 0)
        both = jnp.where(
            rows16 == 0,
            jnp.broadcast_to(ga1[...].astype(WIDE), (16, 16)),
            jnp.where(rows16 == 1, jnp.broadcast_to(ga2[...].astype(WIDE), (16, 16)), 0.0),
        )
        lane_at = ((dp * 4 + slot) % 8) * 16
        spread = jnp.where(iota2((16, 128), 1) == iota2((16, 128), 0) + lane_at, 1.0, 0.0)
        ags[SLOT][c, place, pl.ds(64, 16), :] = low(dot(low(both), low(spread)))
        for t in range(4):
            ags[TILE][t, c, place, pl.ds(0, 64), :] = wu[:, t * 128 : t * 128 + 128]
            ags[TILE][t, c, place, pl.ds(64, 64), :] = wd[:, t * 128 : t * 128 + 128]
        query_w, key_w, value_w, out_w = (
            functools.partial(square_of, ags[n]) for n in (QUERY, KEY, VALUE, OUT_W)
        )

        def up_w(t):
            return tile_of(ags[TILE], t, 0)

        def down_w(t):
            return tile_of(ags[TILE], t, 64)
    else:
        square_v, up_v, down_v = rest
        fw_q, fw_k, fw_v, fw_o, fw_s, fw_u, fw_d, fg1, fg2 = ins_w
        copies = [
            pltpu.make_async_copy(src, dst, lsem.at[4 + i])
            for i, (src, dst) in enumerate((
                (fw_q, square_v.at[0]), (fw_k, square_v.at[1]), (fw_v, square_v.at[2]), (fw_o, square_v.at[3]),
                (fw_s, w_slot), (fw_u, up_v), (fw_d, down_v),
            ))
        ]
        start(copies)
        for copy in copies:
            copy.wait()
        gains[0:1, :] = fg1[...].astype(WIDE)
        gains[1:2, :] = fg2[...].astype(WIDE)
        query_w, key_w, value_w, out_w = (lambda n=n: square_v[n] for n in range(4))

        def up_w(t):
            return up_v[t]

        def down_w(t):
            return down_v[t]

    lane = iota2((CHUNK, LANES), 1)
    sub = iota2((CHUNK, LANES), 0)
    bd_lo[...] = low(jnp.where(lane < 64, 1.0, 0.0))
    bd_hi[...] = low(jnp.where(lane < 64, 0.0, 1.0))
    bdm[...] = jnp.where((lane < 64) == (sub < 64), 1.0, 0.0)
    upper = low(jnp.where(sub <= lane, 1.0, 0.0))
    lower = low(jnp.where(sub >= lane, 1.0, 0.0))
    ones = jnp.ones((CHUNK, LANES), NARROW)
    for n in range(chunks):
        begin = starts_ref[:, pl.ds(pl.multiple_of(half * tokens + n * CHUNK, CHUNK), CHUNK)].astype(WIDE)
        begin = jnp.where(row == 0, begin[0:1], begin[1:2])
        begin = low(jnp.broadcast_to(begin, (CHUNK, LANES)))
        by_lane = dot(begin, upper)
        by_row = dot_nt(lower, begin)
        total = dot(begin, ones)
        same = by_row == by_lane
        v = low(jnp.where(same & (sub >= lane), 1.0, 0.0))
        vt = low(jnp.where(same & (sub <= lane), 1.0, 0.0))
        vis[n, :, 0:128] = v
        vis[n, :, 128:256] = v
        vist[n, :, 0:128] = vt
        vist[n, :, 128:256] = vt
        carried = jnp.where(by_row == 0.0, 1.0, 0.0)
        ending = jnp.where(by_row == total, 1.0, 0.0)
        hcar[n] = carried
        tail[n] = ending
        hcar_n[n] = low(carried)
        tail_n[n] = low(ending)
        passf[n] = jnp.where(total == 0.0, 1.0, 0.0)

    def perm_rows(i, _):
        r = iota2((CHUNK, WIDTH), 0) + i * CHUNK
        n = iota2((CHUNK, WIDTH), 1)
        source = ((n >> 4) & 3) * 128 + (n & 15) * 8 + (n >> 6)
        perm[pl.ds(pl.multiple_of(i * CHUNK, CHUNK), CHUNK), :] = low(jnp.where(r == source, 1.0, 0.0))
        return 0

    lax.fori_loop(0, WIDTH // CHUNK, perm_rows, 0)
    pl.semaphore_wait(barrier, len(peers))

    def gather_steps(*steps):
        if linked:
            for n, stage in steps:
                gather_step(n, stage)

    T0, T1, T2, T3 = range(TILE, TILE + 4)
    gather_steps(*((n, 0) for n in range(9)))
    x_copy.wait()

    def by_chunk(body):
        def step(i, _):
            body(pl.ds(pl.multiple_of(i * CHUNK, CHUNK), CHUNK), i)
            return 0

        lax.fori_loop(0, chunks, step, 0)

    def norm_one(rows, i):
        gtwo[rows, :], _ = norm_parts(x_v[rows, :])

    by_chunk(norm_one)

    if linked:
        gather_steps(
            (SLOT, 1), (KEY, 1), (SLOT, 2), (VALUE, 1), (KEY, 2), (QUERY, 1), (VALUE, 2), (OUT_W, 1), (SLOT, 3),
            (QUERY, 2), (KEY, 3), (T0, 1), (SLOT, 4),
        )
        for index, core, at, odp, oslot in owners(True):
            w_slot[odp * 64 : odp * 64 + 64, oslot * 128 : oslot * 128 + 128] = ags[SLOT][core, at, 0:64, :]
        for window in range(4):
            total = jnp.zeros((16, 128), WIDE)
            for index, core, at, _, _ in owners(True):
                if index // 8 == window:
                    total = total + ags[SLOT][core, at, 64:80, :].astype(WIDE)
            gains[0:8, window * 128 : window * 128 + 128] = total[0:8]
    w_slot[...] = low(dot(w_slot[...], perm[...]))

    gain_one = gains[0:1, :]
    gain_two = gains[1:2, :]

    n1[...] = low(gtwo[...] * gain_one)
    expo[...] = jnp.exp(dot(n1[...], w_slot[...]))
    proj[3] = low(expo[...])
    gather_steps((OUT_W, 2), (VALUE, 3), (KEY, 4))
    proj[1] = low(dot(n1[...], key_w()))
    gather_steps((T1, 1), (QUERY, 3), (VALUE, 4), (T0, 2))
    proj[2] = low(dot(n1[...], value_w()))
    def two(v):
        return jnp.concatenate([v * bd_lo[...], v * bd_hi[...]], axis=0)

    every = range(PAIRS)
    pair_cols = [slice(p * 128, p * 128 + 128) for p in every]

    def local_states(rows, i):
        w_tail = proj[3, rows, :]
        tloc[i] = jnp.broadcast_to(
            dot(jnp.ones((8, CHUNK), NARROW), w_tail * jnp.concatenate([tail_n[i]] * PAIRS, axis=1)),
            (8, WIDTH),
        )
        w = [proj[3, rows, cols] for cols in pair_cols]
        k_tail = [proj[1, rows, cols] * tail_n[i] for cols in pair_cols]
        v = [proj[2, rows, cols] for cols in pair_cols]
        kw = [dot_tn(k_tail[p], w[p]) for p in every]
        wv = [dot_tn(w[p] * tail_n[i], v[p]) for p in every]
        for p in every:
            loc[0, i, p] = kw[p] * bdm[...]
            loc[1, i, p] = wv[p] * bdm[...]

    by_chunk(local_states)

    def scan_states(order, initial, t_initial, keep):
        def one(kind, p):
            state = initial(kind, p)
            for i in order:
                if keep:
                    sin[kind, i, p] = low(state)
                state = loc[kind, i, p] + passf[i] * state
            if not keep:
                xsend[kind, p] = state

        def step(k, _):
            one(k // PAIRS, k % PAIRS)
            return 0

        lax.fori_loop(0, 2 * PAIRS, step, 0)
        state = t_initial()
        for i in order:
            if keep:
                tin[i] = state
            state = tloc[i] + jnp.concatenate([passf[i, 0:8, :]] * PAIRS, axis=1) * state
        if not keep:
            tsend[...] = state

    def exchange(at):
        return [remote(xsend, xrecv.at[(at - STATE) // 2], at, partner), remote(tsend, trecv.at[(at - STATE) // 2], at + 1, partner)]

    def send_states(order, at):
        scan_states(order, lambda k, p: jnp.zeros((128, 128), WIDE), lambda: jnp.zeros((8, WIDTH), WIDE), False)
        start(exchange(at))

    def carry_states(order, at, takes):
        n = (at - STATE) // 2
        recv(exchange(at))
        scan_states(order, lambda k, p: xrecv[n, k, p] * takes, lambda: trecv[n] * takes, True)

    forward = list(range(chunks))
    takes_forward = half.astype(WIDE)
    send_states(forward, STATE)
    gather_steps((OUT_W, 3), (T2, 1), (QUERY, 4))
    proj[0] = low(dot(n1[...], query_w()))
    n1t[...] = n1[...].T
    carry_states(forward, STATE, takes_forward)
    gather_steps((OUT_W, 4), (T1, 2))
    first_half = iota2((CHUNK, LANES), 1) < 64

    def over_heads(lo_part, hi_part):
        return jnp.where(first_half, lo_part, hi_part)

    def head_max(v):
        return over_heads(
            jnp.max(jnp.where(first_half, v, -jnp.inf), axis=-1, keepdims=True),
            jnp.max(jnp.where(first_half, -jnp.inf, v), axis=-1, keepdims=True),
        )

    def head_sum(v):
        return over_heads(
            jnp.sum(jnp.where(first_half, v, 0.0), axis=-1, keepdims=True),
            jnp.sum(jnp.where(first_half, 0.0, v), axis=-1, keepdims=True),
        )

    def attend(rows, i):
        mask = vis[i]
        carried = hcar[i]
        totals = dot(mask[:, 0:128], proj[3, rows, :]) + jnp.concatenate([carried] * PAIRS, axis=1) * tin[i, 0:1, :]
        rtot[rows, :] = 1.0 / totals
        q, k, v, w = ([proj[n, rows, cols] for cols in pair_cols] for n in range(4))
        w2 = [two(w[p]) for p in every]
        cross = [low(dot_nt(q[p], two(k[p]))) * mask for p in every]
        from_state = [dot(q[p], sin[0, i, p]) for p in every]
        numer = [dot(cross[p], w2[p]) for p in every]
        r = [rtot[rows, cols] for cols in pair_cols]
        s = [(numer[p] + carried * from_state[p]) * r[p] for p in every]
        e = [jnp.exp(s[p] - head_max(s[p])) for p in every]
        pr = [e[p] / head_sum(e[p]) for p in every]
        sc = [low(pr[p] * r[p]) for p in every]
        for p in every:
            score[rows, pair_cols[p]] = s[p]
            prob[rows, pair_cols[p]] = pr[p]
            scaled[rows, pair_cols[p]] = sc[p]
        mix = [low(dot_nt(sc[p], w2[p])) * mask for p in every]
        from_state = [dot(sc[p], sin[1, i, p]) for p in every]
        near = [dot(mix[p], two(v[p])) for p in every]
        for p in every:
            att[rows, pair_cols[p]] = low(near[p] + carried * from_state[p])
        if linked:
            for at, steps in ((0, ((T0, 3),)), (1, ((T3, 1),)), (3, ((T2, 2),))):
                pl.when(i == at)(functools.partial(gather_steps, *steps))

    by_chunk(attend)

    mid[...] = x_v[...] + dot(att[...], out_w())
    acc[...] = mid[...]
    cot_copy.wait()

    def norm_two(rows, i):
        xhat, _ = norm_parts(mid[rows, :])
        n2[rows, :] = low(xhat * gain_two)
        gf[rows, :] = low(cot_v[rows, :])
        gtwo[rows, :] = jnp.zeros((CHUNK, WIDTH), WIDE)

    by_chunk(norm_two)
    n2t[...] = n2[...].T
    gft[...] = gf[...].T

    def scatter_steps(*steps):
        if linked:
            for n, stage in steps:
                scatter_step(n, stage, PIECE_ROWS[n])

    def feed(t, _):
        if linked:
            for at, gathered, scattered in (
                (0, ((T1, 3), (T0, 4)), ()),
                (1, ((T3, 2), (T2, 3), (T1, 4)), ((T0, 1),)),
                (2, ((T3, 3), (T2, 4)), ((T1, 1),)),
                (3, ((T3, 4),), ((T0, 2), (T2, 1))),
            ):
                @pl.when(t == at)
                def _(gathered=gathered, scattered=scattered):
                    gather_steps(*gathered)
                    scatter_steps(*scattered)

        hidden = dot(n2[...], up_w(t))
        cdf = 0.5 * (1.0 + lax.erf(hidden * 0.7071067811865476))
        active = low(hidden * cdf)
        slope = cdf + hidden * (jnp.exp(-0.5 * hidden * hidden) * 0.3989422804014327)
        grad_hidden = low(dot(gf[...], down_w(t)) * slope)
        acc[...] += dot_nt(active, down_w(t))
        gtwo[...] += dot_nt(grad_hidden, up_w(t))
        g_up = low(dot(n2t[...], grad_hidden))
        g_down = low(dot(gft[...], active))
        if linked:
            for _, core, at, odp, oslot in owners(False):
                rows, cols = slice(odp * 64, odp * 64 + 64), slice(oslot * 128, oslot * 128 + 128)
                rss[TILE][t, core, at, 0:64, :] = g_up[rows, cols]
                rss[TILE][t, core, at, 64:128, :] = g_down[rows, cols]
            scatter_step(TILE + t, 0, 128)
        else:
            outs[7][t] = g_up
            outs[8][t] = g_down
        return 0

    lax.fori_loop(0, 4, feed, 0)

    mine, theirs = out_ref.at[row, own_rows], out_ref.at[1 - row, own_rows]
    oy, oc, of = remote(outb, mine, OUT, y_peer), remote(outb, mine, OUT + 1, partner), remote(theirs, theirs, OUT + 2, partner)
    ol = pltpu.make_async_copy(outb, mine, lsem.at[2])

    def norm_two_back(rows, i):
        outb[rows, :] = low(acc[rows, :])
        xhat, inv = norm_parts(mid[rows, :])
        up = gtwo[rows, :]
        grad = cot_v[rows, :] + norm_back(xhat, inv, gain_two, up)
        cot_v[rows, :] = grad
        gf[rows, :] = low(grad)
        gains[3:4, :] = gains[3:4, :] + jnp.sum(up * xhat, axis=0, keepdims=True)

    scatter_steps((T3, 1))
    gains[2:8, :] = jnp.zeros((6, WIDTH), WIDE)
    by_chunk(norm_two_back)
    oy.start()
    oc.start()
    ol.start()
    scatter_steps((T0, 3))
    ga[...] = low(dot_nt(gf[...], out_w()))
    g_out = low(dot_tn(att[...], gf[...]))

    def pack_square(n, grad):
        for index, core, at, _, _ in owners(False):
            for t in range(4):
                rss[n][core, at, t * 16 : t * 16 + 16, :] = grad[
                    index * 16 : index * 16 + 16, t * 128 : t * 128 + 128
                ]

    if linked:
        pack_square(OUT_W, g_out)
        scatter_steps((OUT_W, 0))
    else:
        outs[5][...] = g_out

    def back_first(rows, i):
        mask = vis[i]
        carried = hcar[i]
        carried_n = hcar_n[i]
        q, k, v, w = ([proj[n, rows, cols] for cols in pair_cols] for n in range(4))
        g = [ga[rows, cols] for cols in pair_cols]
        w2 = [two(w[p]) for p in every]
        gmix = [low(dot_nt(g[p], two(v[p]))) * mask for p in every]
        from_state = [dot_nt(g[p], sin[1, i, p]) for p in every]
        near = [dot(gmix[p], w2[p]) for p in every]
        r, pr, s = ([ref[rows, cols] for cols in pair_cols] for ref in (rtot, prob, score))
        gs = [low(near[p] + carried * from_state[p]).astype(WIDE) for p in every]
        gp = [gs[p] * r[p] for p in every]
        gscore = [pr[p] * (gp[p] - head_sum(pr[p] * gp[p])) for p in every]
        gn = [low(gscore[p] * r[p]) for p in every]
        gt = [low(-(gp[p] * pr[p] + gscore[p] * s[p]) * r[p]) for p in every]
        for p in every:
            gnum[rows, pair_cols[p]] = gn[p]
            gtot[rows, pair_cols[p]] = gt[p]
        gcross = [low(dot_nt(gn[p], w2[p])) * mask for p in every]
        from_state = [dot_nt(gn[p], sin[0, i, p]) for p in every]
        near = [dot(gcross[p], two(k[p])) for p in every]
        qn = [dot_tn(q[p] * carried_n, gn[p]) for p in every]
        gsc = [dot_tn(g[p] * carried_n, scaled[rows, pair_cols[p]]) for p in every]
        for p in every:
            gproj[0, rows, pair_cols[p]] = low(near[p] + carried * from_state[p])
            loc[0, i, p] = qn[p] * bdm[...]
            loc[1, i, p] = gsc[p] * bdm[...]
        tloc[i] = jnp.broadcast_to(
            dot(
                jnp.ones((8, CHUNK), NARROW),
                jnp.concatenate(gt, axis=1) * jnp.concatenate([carried_n] * PAIRS, axis=1),
            ),
            (8, WIDTH),
        )
        if linked:
            for at, steps in ((0, ((OUT_W, 1),)), (1, ((T1, 2),)), (3, ((T0, 4),))):
                pl.when(i == at)(functools.partial(scatter_steps, *steps))
    by_chunk(back_first)
    sent(exchange(STATE))
    send_states(forward[::-1], BACK)
    grad = low(dot(n1t[...], gproj[0]))
    if linked:
        pack_square(QUERY, grad)
        scatter_steps((QUERY, 0))
    else:
        outs[2][...] = grad
    carry_states(forward[::-1], BACK, 1.0 - takes_forward)
    def spread_gin(i):
        part = pl.ds(pl.multiple_of(half * tokens + i * CHUNK, CHUNK), CHUNK)
        mine, theirs, at = gin_ref.at[row, part], gin_ref.at[1 - row, part], GIN + 3 * i
        source = ginb.at[pl.ds(pl.multiple_of(i * CHUNK, CHUNK), CHUNK)]
        return remote(source, mine, at, y_peer), remote(source, mine, at + 1, partner), remote(theirs, theirs, at + 2, partner)

    def back_second(rows, i):
        mask = vist[i]
        ends = tail[i]
        wc = dot(mask[:, 0:128], gtot[rows, :]) + jnp.concatenate([ends] * PAIRS, axis=1) * tin[i, 0:1, :]
        q, k, v, w = ([proj[n, rows, cols] for cols in pair_cols] for n in range(4))
        g, sc, gn = ([ref[rows, cols] for cols in pair_cols] for ref in (ga, scaled, gnum))
        g2, sc2, gn2, q2 = ([two(m[p]) for p in every] for m in (g, sc, gn, q))
        s_query, s_grad = ([sin[n, i, p] for p in every] for n in range(2))
        mix = [low(dot_nt(w[p], sc2[p])) * mask for p in every]
        gmix = [low(dot_nt(v[p], g2[p])) * mask for p in every]
        cross = [low(dot_nt(k[p], q2[p])) * mask for p in every]
        gcross = [low(dot_nt(w[p], gn2[p])) * mask for p in every]
        from_state = [dot_nt(w[p], s_grad[p]) for p in every]
        near = [dot(mix[p], g2[p]) for p in every]
        for p in every:
            gproj[2, rows, pair_cols[p]] = low(near[p] + ends * from_state[p])
        from_state = [dot_nt(w[p], s_query[p]) for p in every]
        near = [dot(gcross[p], q2[p]) for p in every]
        for p in every:
            gproj[1, rows, pair_cols[p]] = low(near[p] + ends * from_state[p])
        from_state = [dot(v[p], s_grad[p]) + dot(k[p], s_query[p]) for p in every]
        near = [dot(gmix[p], sc2[p]) + dot(cross[p], gn2[p]) for p in every]
        for p in every:
            gw = low(near[p] + ends * from_state[p] + wc[:, pair_cols[p]]).astype(WIDE)
            gproj[3, rows, pair_cols[p]] = low(gw * expo[rows, pair_cols[p]])
        up = dot_nt(gproj[0, rows, :], query_w()) + dot_nt(gproj[1, rows, :], key_w())
        up = up + dot_nt(gproj[2, rows, :], value_w()) + dot_nt(gproj[3, rows, :], w_slot[...])
        xhat, inv = norm_parts(x_v[rows, :])
        ginb[rows, :] = low(cot_v[rows, :] + norm_back(xhat, inv, gain_one, up))
        gains[2:3, :] = gains[2:3, :] + jnp.sum(up * xhat, axis=0, keepdims=True)
        if linked:
            for at, steps in (
                (0, ((QUERY, 1), (T2, 2), (T1, 3))), (2, ((T3, 2),)), (3, ((OUT_W, 2), (T2, 3)))
            ):
                pl.when(i == at)(functools.partial(scatter_steps, *steps))
        iy, ic = spread_gin(i)[:2]
        iy.start()
        ic.start()

        @pl.when(i == 1)
        def _():
            oy.wait_recv()
            of.start()


    by_chunk(back_second)

    il = pltpu.make_async_copy(ginb, gin_ref.at[row, own_rows], lsem.at[3])
    il.start()
    for n, piece in ((2, VALUE), (1, KEY), (3, SLOT)):
        grad = low(dot(n1t[...], gproj[n]))
        if n == 3:
            grad = low(dot_nt(grad, perm[...]))
        if not linked:
            outs[2 + n if n < 3 else 6][...] = grad
        elif n < 3:
            pack_square(piece, grad)
        else:
            for index, core, at, odp, oslot in owners(False):
                rss[SLOT][core, at, 0:64, :] = grad[odp * 64 : odp * 64 + 64, oslot * 128 : oslot * 128 + 128]
                window = index // 8
                rss[SLOT][core, at, 64:80, :] = low(
                    jnp.concatenate(
                        [gains[2:4, window * 128 : window * 128 + 128], jnp.zeros((14, 128), WIDE)], axis=0
                    )
                )
        scatter_steps((piece, 0))
    def forward_gin(i):
        _, _, if_ = spread_gin(i)
        spread_gin(i)[0].wait_recv()
        if_.start()

    scatter_steps((T1, 4), (QUERY, 2), (VALUE, 1))
    forward_gin(0)
    scatter_steps((KEY, 1), (T2, 4))
    forward_gin(1)
    scatter_steps((SLOT, 1), (T3, 3), (OUT_W, 3))
    forward_gin(2)
    scatter_steps((VALUE, 2), (KEY, 2))
    forward_gin(3)
    scatter_steps((SLOT, 2), (T3, 4), (OUT_W, 4), (QUERY, 3), (VALUE, 3), (KEY, 3))
    scatter_steps((QUERY, 4), (SLOT, 3), (VALUE, 4), (KEY, 4))
    scatter_steps((SLOT, 4))
    if not linked:
        outs[9][...] = gains[2:4, :]

    oc.wait()
    oy.wait_send()
    ol.wait()
    of.wait()
    il.wait()
    for i in range(chunks):
        iy, ic, if_ = spread_gin(i)
        iy.wait_send()
        ic.wait()
        if_.wait()
    sent(exchange(BACK))
    if linked:
        for n in range(9):
            sent(gather_z(n) + gather_b(n) + gather_a(n) + gather_last(n))
            for stage in range(4):
                sent(scatter_copies(n, stage))


def finish_kernel(out_ref, gin_ref, small_ref, o, g, gq, gk, gv, go, gs, gu, gd, g1, g2):
    o[...] = out_ref[...].astype(WIDE)
    g[...] = gin_ref[...].astype(WIDE)

    @pl.when(pl.program_id(0) == 0)
    def _():
        base = 0
        bases = []
        for rows in PIECE_ROWS:
            bases.append(base)
            base += rows
        gs[...] = small_ref[0:64, :]
        mine = lax.axis_index("dp") * lax.axis_size("slot") + lax.axis_index("slot")
        window = small_ref[64:72, :]
        lanes = iota2((8, 128), 1)
        first = (mine % 8) * 16
        moved = jnp.concatenate(
            [
                jnp.sum(jnp.where(lanes == first + k, window, 0.0), axis=1, keepdims=True)
                for k in range(16)
            ],
            axis=1,
        )
        g1[...] = moved[0:1]
        g2[...] = moved[1:2]
        for t in range(4):
            cols = slice(t * 128, t * 128 + 128)
            for n, target in ((QUERY, gq), (KEY, gk), (VALUE, gv), (OUT_W, go)):
                target[:, cols] = small_ref[bases[n] + t * 16 : bases[n] + t * 16 + 16, :]
            gu[:, cols] = small_ref[bases[TILE + t] : bases[TILE + t] + 64, :]
            gd[:, cols] = small_ref[bases[TILE + t] + 64 : bases[TILE + t] + 128, :]


def finish(out, gin, small):
    rows, length, width = out.shape
    block = pl.BlockSpec((1, 512, width), lambda i: (i // (length // 512), i % (length // 512), 0))
    whole = lambda shape: pl.BlockSpec(shape, lambda i: (0,) * len(shape))
    shapes = [(16, width)] * 4 + [(64, 128), (64, width), (64, width), (1, 16), (1, 16)]
    shape = jax.ShapeDtypeStruct
    return pl.pallas_call(
        finish_kernel,
        grid=(rows * length // 512,),
        out_shape=[shape(out.shape, WIDE)] * 2 + [shape(s, WIDE) for s in shapes],
        in_specs=[block, block, whole(small.shape)],
        out_specs=[block, block] + [whole(s) for s in shapes],
        compiler_params=pltpu.CompilerParams(vmem_limit_bytes=60 * 1024 * 1024),
    )(out, gin, small)


def run_block(linked, inputs, starts, cotangent, weights):
    rows, length, width = inputs.shape
    tokens = length // 2
    chunks = tokens // CHUNK
    vm = pltpu.VMEM
    scratch = [
        vm((tokens, width), WIDE), vm((tokens, width), WIDE),
        vm((width, width), NARROW), vm((width, width), NARROW), vm((8, width), WIDE),
        vm((tokens, width), NARROW), vm((width, tokens), NARROW),
        vm((4, tokens, width), NARROW), vm((tokens, width), WIDE),
        vm((tokens, width), WIDE), vm((tokens, width), WIDE), vm((tokens, width), WIDE),
        vm((tokens, width), NARROW), vm((tokens, width), NARROW),
        vm((tokens, width), WIDE), vm((tokens, width), WIDE),
        vm((tokens, width), NARROW), vm((width, tokens), NARROW),
        vm((tokens, width), NARROW), vm((width, tokens), NARROW), vm((tokens, width), WIDE),
        vm((tokens, width), NARROW), vm((4, tokens, width), NARROW),
        vm((tokens, width), NARROW), vm((tokens, width), NARROW),
        vm((tokens, width), NARROW), vm((tokens, width), NARROW),
        vm((chunks, CHUNK, 256), NARROW), vm((chunks, CHUNK, 256), NARROW),
        vm((chunks, CHUNK, LANES), WIDE), vm((chunks, CHUNK, LANES), WIDE), vm((chunks, CHUNK, LANES), WIDE),
        vm((chunks, CHUNK, LANES), NARROW), vm((chunks, CHUNK, LANES), NARROW),
        vm((2, chunks, PAIRS, 128, 128), WIDE), vm((2, chunks, PAIRS, 128, 128), NARROW),
        vm((chunks, 8, width), WIDE), vm((chunks, 8, width), WIDE),
        vm((CHUNK, LANES), NARROW), vm((CHUNK, LANES), NARROW), vm((CHUNK, LANES), WIDE),
        vm((2, PAIRS, 128, 128), WIDE), vm((2, 2, PAIRS, 128, 128), WIDE),
        vm((8, width), WIDE), vm((2, 8, width), WIDE),
        pltpu.SemaphoreType.DMA((152,)), pltpu.SemaphoreType.DMA((152,)), pltpu.SemaphoreType.DMA((12,)),
    ]
    if linked:
        for lead in ((2, 16), (2, 16), (16,), (8,), (4,), (3,)):
            scratch += [vm((*lead, r, LANES), NARROW) for r in PIECE_ROWS[:TILE]]
            scratch += [vm((4, *lead, 128, LANES), NARROW)]
    else:
        scratch += [vm((4, width, width), NARROW)] * 3
    anywhere = pl.BlockSpec(memory_space=pl.ANY)
    here = pl.BlockSpec(memory_space=pltpu.VMEM)
    shape = jax.ShapeDtypeStruct
    big = [shape((rows, length, width), NARROW)] * 2
    square = (width, width)
    if linked:
        small = [shape((SMALL_ROWS, LANES), WIDE)]
        weight_specs = [here] * 9
    else:
        small = [shape(square, NARROW)] * 5 + [shape((4, *square), NARROW)] * 2 + [shape((2, width), WIDE)]
        weight_specs = [anywhere] * 7 + [here] * 2
    return pl.pallas_call(
        functools.partial(block_kernel, linked, 12, 2 + len(small)),
        out_shape=big + small,
        in_specs=[anywhere, here, anywhere] + weight_specs,
        out_specs=[anywhere] * 2 + [here] * len(small),
        scratch_shapes=scratch,
        compiler_params=pltpu.CompilerParams(
            collective_id=0, has_side_effects=True, vmem_limit_bytes=62 * 1024 * 1024
        ),
    )(inputs, starts, cotangent, *weights)


def on_device(
    inputs, starts, w_query, w_key, w_value, w_out, w_slot, w_up, w_down, gain_attn, gain_ffn, cotangent
):
    n_dp, n_slot = lax.axis_size("dp"), lax.axis_size("slot")
    if n_dp == 8 and n_slot == 4:
        weights = (
            w_query, w_key, w_value, w_out, w_slot, w_up, w_down.T,
            gain_attn.reshape(1, -1), gain_ffn.reshape(1, -1),
        )
        out, gin, small = run_block(True, inputs, starts, cotangent, weights)
        out, gin, gq, gk, gv, go, gs, gu, gd, g1, g2 = finish(out, gin, small)
        return out, gin, gq, gk, gv, go, gs, gu, gd.T, g1.reshape(-1), g2.reshape(-1)

    def whole(v, names, axis):
        return lax.all_gather(v, names, axis=axis, tiled=True)

    both = ("dp", "slot")
    width = inputs.shape[-1]
    up = whole(whole(w_up, "dp", 0), "slot", 1).reshape(width, 4, 4, 128).transpose(2, 0, 1, 3)
    down = whole(whole(w_down, "dp", 1), "slot", 0).reshape(4, 4, 128, width).transpose(1, 3, 0, 2)
    up, down = up.reshape(4, width, width), down.reshape(4, width, width)
    weights = (
        whole(w_query, both, 0), whole(w_key, both, 0), whole(w_value, both, 0), whole(w_out, both, 0),
        whole(whole(w_slot, "dp", 0), "slot", 1), up, down,
        whole(gain_attn, both, 0).reshape(1, -1), whole(gain_ffn, both, 0).reshape(1, -1),
    )
    out, gin, gq, gk, gv, go, gs, gu, gd, gg = run_block(False, inputs, starts, cotangent, weights)

    def shared(v, names, axis):
        return lax.psum_scatter(v.astype(WIDE), names, scatter_dimension=axis, tiled=True)

    gu = gu.reshape(4, width, 4, 128).transpose(1, 2, 0, 3).reshape(width, -1)
    gd = gd.reshape(4, width, 4, 128).transpose(2, 0, 3, 1).reshape(-1, width)
    return (
        out.astype(WIDE), gin.astype(WIDE),
        shared(gq, both, 0), shared(gk, both, 0), shared(gv, both, 0), shared(go, both, 0),
        shared(shared(gs, "slot", 1), "dp", 0), shared(shared(gu, "slot", 1), "dp", 0),
        shared(shared(gd, "slot", 0), "dp", 1), shared(gg[0], both, 0), shared(gg[1], both, 0),
    )


def solution(mesh):
    every = ("dp", "slot")
    rows = P("dp", None, None)
    return jax.shard_map(
        on_device,
        mesh=mesh,
        in_specs=(
            rows, P("dp", None), P(every, None), P(every, None), P(every, None), P(every, None),
            P("dp", "slot"), P("dp", "slot"), P("slot", "dp"), P(every), P(every), rows,
        ),
        out_specs=(
            rows, rows, P(every, None), P(every, None), P(every, None), P(every, None),
            P("dp", "slot"), P("dp", "slot"), P("slot", "dp"), P(every), P(every),
        ),
        check_vma=False,
    )
```

time: 150 us -> 111 us (0.74)
  Pallas kernels: 135 us -> 110 us
  local copies, waits for them, and re-layouts: 7.43 us -> 0 us
  other arithmetic: 6.81 us -> 0 us
    pallas_call x1, Pallas kernels: 135 us -> 104 us  [run_block(): pl.pallas_call(functools.partial(block_kernel, linked, 12, 2 + len(small)...]
    convert_element_type x2 -> x0, other arithmetic: 6.81 us -> none  [the longest x1 4.2 us: on_device(): out.astype(WIDE)]
    pallas_call x0 -> x1, Pallas kernels: none -> 6.33 us  [finish(): pl.pallas_call(finish_kernel, grid=(rows * length // 512,), out_shape=[sh...]
    unnamed x24 -> x0, local copies, waits for them, and re-layouts: 6.02 us -> none
where the time goes in v2:
time: 111 us; the launch traced here: 110 us
  Pallas kernels  110 us (99%)
    pallas_call x1, Pallas kernels, run_block(): pl.pallas_call(functools.partial(block_kernel, linked, 12, 2 + len(small)...  104 us
    pallas_call x1, Pallas kernels, finish(): pl.pallas_call(finish_kernel, grid=(rows * length // 512,), out_shape=[sh...  6.33 us

profile of v2, /device:TPU:0, one launch (start us, length us, event | category | flops | bytes accessed | tf_op | source)
XLA Modules:
  0.0 110.5 jit_solution(10048445850177337359)
XLA Ops:
  0.6 103.5 %shard_map.203 = (bf16[2,1024,512]{2,1,0:T(8,128)(2,1)}, bf16[2,1024,512]{2,1,0:T(8,128)(2,1)}, f32[848,128]{1,0:T(8,128)}) custom-call(f32[2,1024,512]{2,1,0:T(8,128)} %refs_0_.1, s32[2,1024]{1,0:T(2,128)} %refs_1_.1, f32[2,1024,512]{2,1,0:T(8,128)} %refs_2_.1, bf16[16,512]{1,0:T(8,128)(2,1)} %refs_3_.1, bf16[16,512]{1,0:T(8,128)(2,1)} %refs_4_.1, ...), custom_call_target="tpu_custom_call" | custom-call | tf_op jit(solution)/shard_map/pallas_call | solution.py:826
  104.2 6.3 %shard_map.204 = (f32[2,1024,512]{2,1,0:T(8,128)}, f32[2,1024,512]{2,1,0:T(8,128)}, f32[16,512]{1,0:T(8,128)}, f32[16,512]{1,0:T(8,128)}, f32[16,512]{1,0:T(8,12...) custom-call(bf16[2,1024,512]{2,1,0:T(8,128)(2,1)} %get-tuple-element, ...), custom_call_target="tpu_custom_call" | custom-call | tf_op jit(solution)/shard_map/pallas_call | solution.py:771

commit v3 on v2

--- a/solution.py
+++ b/solution.py
@@ -20,7 +20,47 @@
 PIECE_ROWS = (80, 64, 64, 64, 64, 128, 128, 128, 128)
 SLOT, KEY, VALUE, QUERY, OUT_W, TILE = range(6)
 SMALL_ROWS = sum(PIECE_ROWS)
-GATHER_SEMS, SCATTER_SEMS = 8, 6
+GATHER_MODES = (
+    ("ABZ", "m"), ("ABZ", "m"), ("ABZ", "m"), ("ABZ", "m"), ("ABZ", "m"),
+    ("ABZ", "m"), ("ABZ", "m"), ("ABZ", "m"), ("ABZ", "m"),
+)
+SCATTER_MODES = (
+    ("ABZ", "x"), ("ABZ", "m"), ("ABZ", "x"), ("AZB", "x"), ("ABZ", "m"),
+    ("ABZ", "m"), ("AZB", "m"), ("AZB", "x"), ("ABZ", "x"),
+)
+PLAN = {
+    "slot": ("S1", "K1", "V1", "S2", "K2", "Q1", "V2", "O1", "S3", "K3", "T01", "Q2", "S4",),
+    "key": ("V3", "K4", "O2",),
+    "val": ("V4",),
+    "loc": ("T11", "Q3", "T02",),
+    "qry": ("Q4", "O3",),
+    "scan": ("O4", "T21",),
+    "att0": ("T12",),
+    "att3": ("T31",),
+    "outp": ("T03", "T22",),
+    "ffn0a": ("T13", "T04",),
+    "ffn0b": ("T32",),
+    "ffn1a": ("T14",),
+    "ffn1b": ("T23",),
+    "ffn2a": ("T0.1", "T24",),
+    "ffn2b": ("T33",),
+    "ffn3a": ("T1.1", "T34",),
+    "n2b": ("T0.2",),
+    "ga": ("T2.1",),
+    "gout": ("T1.2",),
+    "B1_2": ("O.0",),
+    "scan2": ("T0.3", "T3.1", "Q.0", "T2.2", "O.1",),
+    "B2_1": ("y0",),
+    "B2_2": ("V.0", "y1", "Q.1",),
+    "B2_3": ("V.1", "O.2", "T3.2",),
+    "wS": ("K.0", "Q.2",),
+    "end": (
+        "S.0", "K.1", "V.2", "O.3", "y2", "S.1", "K.2", "T3.3", "Q.3", "V.3", "S.2", "f0", "T2.3", "T0.4",
+        "T1.3", "K.3", "y3", "f", "T3.4", "f2", "V.4", "S.3", "T1.4", "T2.4", "Q.4", "K.4", "O.4", "f1",
+        "S.4", "f3",
+    ),
+}
+SEMS = 4
 
 
 def dot(a, b):
@@ -58,28 +98,36 @@
     return (u - row_mean(u) - xhat * row_mean(u * xhat)) * inv
 
 
-def owners(mixed):
+def strides(mode):
+    sizes = tuple(4 if axis == "Z" else 2 for axis in mode[0])
+    return sizes, (sizes[1] * sizes[2], sizes[2], 1)
+
+
+def owners(mode):
     out = []
+    _, steps = strides(mode)
     for dp in range(8):
         for slot in range(4):
             z, x, y, c = dp // 2, dp % 2, slot // 2, slot % 2
-            a, b = (y, x) if c == 0 and mixed else (x, y)
-            out.append((dp * 4 + slot, c, a * 8 + b * 4 + z, dp, slot))
+            first_y = mode[1] == "y" or (mode[1] == "m" and c == 0)
+            at = {"A": y if first_y else x, "B": x if first_y else y, "Z": z}
+            place = sum(at[axis] * step for axis, step in zip(mode[0], steps))
+            out.append((dp * 4 + slot, c, place, dp, slot))
     return out
 
 
-def square_of(buf):
+def square_of(buf, n):
     return jnp.concatenate(
         [
             jnp.concatenate([buf[core, at, t * 16 : t * 16 + 16, :] for t in range(4)], axis=1)
-            for _, core, at, _, _ in owners(True)
+            for _, core, at, _, _ in owners(GATHER_MODES[n])
         ],
         axis=0,
     )
 
 
 def tile_of(buf, n, first):
-    place = {(dp, slot): (core, at) for _, core, at, dp, slot in owners(True)}
+    place = {(dp, slot): (core, at) for _, core, at, dp, slot in owners(GATHER_MODES[TILE])}
     return jnp.concatenate(
         [
             jnp.concatenate(
@@ -110,15 +158,20 @@
     partner = (dp, y * 2 + (1 - c))
     y_peer = (dp, (1 - y) * 2 + c)
     if linked:
-        ags, rss, rcs, ras, rbs, rzs = (rest[6 * n : 6 * n + 6] for n in range(6))
+        ags, rss, rcs = (rest[6 * n : 6 * n + 6] for n in range(3))
+        got_refs = [rest[18 + 9 * n : 27 + 9 * n] for n in range(3)]
         z, x = dp // 2, dp % 2
-        xa = y + c * (x - y)
-        xb = x + c * (y - x)
-        place = xa * 8 + xb * 4 + z
-        own = x * 8 + y * 4 + z
         x_peer = (z * 2 + 1 - x, slot)
-        dev_a = ((z * 2 + x + c * (1 - 2 * x)), slot + (1 - c) * 2 * (1 - 2 * y))
-        dev_b = ((z * 2 + x + (1 - c) * (1 - 2 * x)), slot + c * 2 * (1 - 2 * y))
+        near = {
+            "x": (x, y, x_peer, y_peer),
+            "y": (y, x, y_peer, x_peer),
+            "m": (
+                y + c * (x - y),
+                x + c * (y - x),
+                (z * 2 + x + c * (1 - 2 * x), slot + (1 - c) * 2 * (1 - 2 * y)),
+                (z * 2 + x + (1 - c) * (1 - 2 * x), slot + c * 2 * (1 - 2 * y)),
+            ),
+        }
         z_peers = [((((z + s) % 4) * 2 + x), slot) for s in (1, 2, 3)]
         peers = [partner, x_peer, y_peer] + z_peers
     else:
@@ -134,9 +187,9 @@
     x_copy.start()
     cot_copy.start()
 
-    def remote(src, dst, at, device):
+    def remote(src, dst, at, device, send_at=None):
         return pltpu.make_async_remote_copy(
-            src_ref=src, dst_ref=dst, send_sem=ssem.at[at], recv_sem=rsem.at[at],
+            src_ref=src, dst_ref=dst, send_sem=ssem.at[at if send_at is None else send_at], recv_sem=rsem.at[at],
             device_id=device, device_id_type=MESH,
         )
 
@@ -155,89 +208,120 @@
     def view(bufs, n):
         return bufs[n] if isinstance(n, int) and n < TILE else bufs[TILE].at[n - TILE]
 
-    def gather_z(n):
-        mine, at = view(ags, n).at[c, place], n * GATHER_SEMS
-        return [remote(mine, mine, at + s, z_peers[s]) for s in range(3)]
-
-    def gather_b(n):
-        part, at = view(ags, n).at[c, pl.ds(xa * 8 + xb * 4, 4)], n * GATHER_SEMS
-        return [remote(part, part, at + 3, dev_b), remote(part, part, at + 5, partner)]
-
-    def gather_a(n):
-        buf, at = view(ags, n), n * GATHER_SEMS
-        part = buf.at[c, pl.ds(xa * 8, 8)]
-        other = buf.at[c, pl.ds(xa * 8 + (1 - xb) * 4, 4)]
-        return [remote(part, part, at + 4, dev_a), remote(other, other, at + 6, partner)]
-
-    def gather_last(n):
-        part = view(ags, n).at[c, pl.ds((1 - xa) * 8, 8)]
-        return [remote(part, part, n * GATHER_SEMS + 7, partner)]
+    def mode_of(modes, n):
+        return modes[n if isinstance(n, int) else TILE]
+
+    def axes(mode):
+        pa, pb, dev_a, dev_b = near[mode[1]]
+        known = {
+            "A": (pa, [(1 - pa, dev_a)]),
+            "B": (pb, [(1 - pb, dev_b)]),
+            "Z": (z, [((z + s + 1) % 4, z_peers[s]) for s in range(3)]),
+        }
+        return [(known[axis][0], step, known[axis][1]) for axis, step in zip(mode[0], strides(mode)[1])]
+
+    def place_in(mode, upto=3):
+        return sum(at * step for at, step, _ in axes(mode)[:upto])
+
+    def gather_along(n, k):
+        mode = mode_of(GATHER_MODES, n)
+        _, step, others = axes(mode)[k]
+        part = view(ags, n).at[c, pl.ds(place_in(mode, k + 1), step)]
+        return [remote(part, part, n * SEMS + k, device) for _, device in others]
+
+    def gather_along_all(n, k):
+        _, step, others = axes(mode_of(GATHER_MODES, n))[k]
+        part = view(ags, n).at[c, pl.ds(0, step * len(others))]
+        return remote(part, part, n * SEMS + k, partner)
+
+    def gather_across(n, k):
+        mode = mode_of(GATHER_MODES, n)
+        _, step, others = axes(mode)[k]
+        base = place_in(mode, k)
+        if k == 2:
+            parts = [pl.ds(base, strides(mode)[0][2])]
+        else:
+            parts = [pl.ds(base + place * step, step) for place, _ in others]
+        refs = [view(ags, n).at[c, part] for part in parts]
+        return [remote(ref, ref, n * SEMS + 3, partner) for ref in refs]
+
+    def gather_across_all(n):
+        every_block = view(ags, n).at[c]
+        return remote(every_block, every_block, n * SEMS + 3, partner)
 
     def gather_step(n, stage):
+        if stage == 4:
+            gather_across_all(n).wait_recv()
+            return
+        if stage:
+            gather_along_all(n, 3 - stage).wait_recv()
+        if stage < 3:
+            start(gather_along(n, 2 - stage))
+        if stage:
+            start(gather_across(n, 3 - stage))
+
+    def gather_sent(n):
+        sent([gather_along_all(n, k) for k in range(3)] + [gather_across_all(n)])
+
+    def scatter_copies(n, stage):
+        buf, at, send = view(rss, n), SCATTER + n * SEMS + stage, n * SEMS + stage
         if stage == 0:
-            start(gather_z(n))
-        elif stage == 1:
-            recv(gather_z(n))
-            start(gather_b(n))
-        elif stage == 2:
-            recv(gather_b(n)[:1])
-            start(gather_a(n))
-        elif stage == 3:
-            recv(gather_a(n)[:1])
-            start(gather_last(n))
-        else:
-            recv(gather_b(n)[1:] + gather_a(n)[1:] + gather_last(n))
-
-    def scatter_copies(n, stage):
-        buf, at = view(rss, n), SCATTER + n * SCATTER_SEMS
+            return [remote(buf.at[1 - c], view(rcs, n), at, partner, send)]
+        mode = SCATTER_MODES[n]
+        _, step, others = axes(mode)[stage - 1]
+        base, got = place_in(mode, stage - 1), got_refs[stage - 1][n]
+        return [
+            remote(buf.at[c, pl.ds(base + place * step, step)], got.at[pl.ds(i * step, step)], at, device, send)
+            for i, (place, device) in enumerate(others)
+        ]
+
+    def scatter_all(n, stage):
         if stage == 0:
-            return [remote(buf.at[1 - c], view(rcs, n), at, partner)]
-        if stage == 1:
-            return [remote(buf.at[c, pl.ds((1 - x) * 8, 8)], view(ras, n), at + 1, x_peer)]
-        if stage == 2:
-            return [remote(buf.at[c, pl.ds(x * 8 + (1 - y) * 4, 4)], view(rbs, n), at + 2, y_peer)]
-        got = view(rzs, n)
-        return [
-            remote(buf.at[c, x * 8 + y * 4 + (z + s + 1) % 4], got.at[s], at + 3 + s, z_peers[s])
-            for s in range(3)
-        ]
+            return scatter_copies(n, stage)[0]
+        got = got_refs[stage - 1][n]
+        part = view(rss, n).at[c, pl.ds(0, got.shape[0])]
+        return remote(part, got, SCATTER + n * SEMS + stage, partner, n * SEMS + stage)
 
     def scatter_step(n, stage, rows):
         if stage:
-            recv(scatter_copies(n, stage - 1))
-            buf = view(rss, n)
+            scatter_all(n, stage - 1).wait_recv()
+            buf, mode = view(rss, n), SCATTER_MODES[n]
+            got = view(rcs, n) if stage == 1 else got_refs[stage - 2][n]
+            count = 16 if stage == 1 else axes(mode)[stage - 2][1]
+            first, terms = place_in(mode, stage - 1), got.shape[0] // count
+
+            def summed(i):
+                total = buf[c, first + i].astype(WIDE)
+                for k in range(terms):
+                    total = total + got[k * count + i].astype(WIDE)
+                return total
+
             if stage < 4:
-                got = view((rcs, ras, rbs)[stage - 1], n)
-                first, count = ((0, 16), (x * 8, 8), (x * 8 + y * 4, 4))[stage - 1]
-
                 def step(i, _):
-                    at = first + i
-                    buf[c, at] = low(buf[c, at].astype(WIDE) + got[i].astype(WIDE))
+                    buf[c, first + i] = low(summed(i))
                     return 0
 
                 lax.fori_loop(0, count, step, 0)
             else:
-                got = view(rzs, n)
-                total = buf[c, own].astype(WIDE)
-                for s in range(3):
-                    total = total + got[s].astype(WIDE)
-                base = sum(PIECE_ROWS[:n]) if isinstance(n, int) else sum(PIECE_ROWS[:TILE]) + (n - TILE) * 128
-                small_ref[pl.ds(base, rows), :] = total
+                small_ref[pl.ds(sum(PIECE_ROWS[:n]), rows), :] = summed(0)
+        else:
+            gather_sent(n)
         if stage < 4:
             start(scatter_copies(n, stage))
 
-    SCATTER = 9 * GATHER_SEMS
-    STATE = SCATTER + 9 * SCATTER_SEMS
+    SCATTER = 9 * SEMS
+    STATE = SCATTER + 9 * SEMS
     BACK, OUT, GIN = STATE + 2, STATE + 4, STATE + 7
 
     ins_w = ins[3:]
     if linked:
         small_ref = outs[2]
         wq, wk, wv, wo, ws, wu, wd, ga1, ga2 = ins_w
+        place = [place_in(mode) for mode in GATHER_MODES]
         for n, shard in ((QUERY, wq), (KEY, wk), (VALUE, wv), (OUT_W, wo)):
             for t in range(4):
-                ags[n][c, place, pl.ds(t * 16, 16), :] = shard[:, t * 128 : t * 128 + 128]
-        ags[SLOT][c, place, pl.ds(0, 64), :] = ws[...]
+                ags[n][c, place[n], pl.ds(t * 16, 16), :] = shard[:, t * 128 : t * 128 + 128]
+        ags[SLOT][c, place[SLOT], pl.ds(0, 64), :] = ws[...]
         rows16 = iota2((16, 16), 0)
         both = jnp.where(
             rows16 == 0,
@@ -246,12 +330,12 @@
         )
         lane_at = ((dp * 4 + slot) % 8) * 16
         spread = jnp.where(iota2((16, 128), 1) == iota2((16, 128), 0) + lane_at, 1.0, 0.0)
-        ags[SLOT][c, place, pl.ds(64, 16), :] = low(dot(low(both), low(spread)))
+        ags[SLOT][c, place[SLOT], pl.ds(64, 16), :] = low(dot(low(both), low(spread)))
         for t in range(4):
-            ags[TILE][t, c, place, pl.ds(0, 64), :] = wu[:, t * 128 : t * 128 + 128]
-            ags[TILE][t, c, place, pl.ds(64, 64), :] = wd[:, t * 128 : t * 128 + 128]
+            ags[TILE][t, c, place[TILE], pl.ds(0, 64), :] = wu[:, t * 128 : t * 128 + 128]
+            ags[TILE][t, c, place[TILE], pl.ds(64, 64), :] = wd[:, t * 128 : t * 128 + 128]
         query_w, key_w, value_w, out_w = (
-            functools.partial(square_of, ags[n]) for n in (QUERY, KEY, VALUE, OUT_W)
+            functools.partial(square_of, ags[n], n) for n in (QUERY, KEY, VALUE, OUT_W)
         )
 
         def up_w(t):
@@ -282,6 +366,61 @@
         def down_w(t):
             return down_v[t]
 
+    pl.semaphore_wait(barrier, len(peers))
+
+    mine, theirs = out_ref.at[row, own_rows], out_ref.at[1 - row, own_rows]
+    oy, oc, of = remote(outb, mine, OUT, y_peer), remote(outb, mine, OUT + 1, partner), remote(theirs, theirs, OUT + 2, partner)
+    ol = pltpu.make_async_copy(outb, mine, lsem.at[2])
+
+    def spread_gin(i):
+        part = pl.ds(pl.multiple_of(half * tokens + i * CHUNK, CHUNK), CHUNK)
+        mine, theirs = gin_ref.at[row, part], gin_ref.at[1 - row, part]
+        source = ginb.at[pl.ds(pl.multiple_of(i * CHUNK, CHUNK), CHUNK)]
+        return (
+            remote(source, mine, GIN + i, y_peer),
+            remote(source, mine, GIN + chunks, partner),
+            remote(theirs, theirs, GIN + chunks + 1, partner),
+        )
+
+    def spread_gin_all(k):
+        mine = gin_ref.at[row, own_rows]
+        return remote(mine, mine, GIN + chunks + k, partner)
+
+    def spread_steps(word):
+        if word == "f":
+            oy.wait_recv()
+            of.start()
+            return
+        sends = spread_gin(int(word[1]))
+        if word[0] == "y":
+            sends[0].start()
+            sends[1].start()
+        else:
+            sends[0].wait_recv()
+            sends[2].start()
+
+    names = {"S": SLOT, "K": KEY, "V": VALUE, "Q": QUERY, "O": OUT_W}
+    names.update({"T%d" % t: TILE + t for t in range(4)})
+
+    def planned(block):
+        for word in PLAN.get(block, ()):
+            if word[0] in "yf":
+                spread_steps(word)
+            elif linked:
+                if "." in word:
+                    piece, stage = word.split(".")
+                    scatter_step(names[piece], int(stage), PIECE_ROWS[names[piece]])
+                else:
+                    gather_step(names[word[:-1]], int(word[-1]))
+
+    def planned_at(block, i):
+        for k in range(4):
+            if PLAN.get(block % k):
+                pl.when(i == k)(functools.partial(planned, block % k))
+
+    if linked:
+        for n in range(9):
+            gather_step(n, 0)
     lane = iota2((CHUNK, LANES), 1)
     sub = iota2((CHUNK, LANES), 0)
     bd_lo[...] = low(jnp.where(lane < 64, 1.0, 0.0))
@@ -320,15 +459,6 @@
         return 0
 
     lax.fori_loop(0, WIDTH // CHUNK, perm_rows, 0)
-    pl.semaphore_wait(barrier, len(peers))
-
-    def gather_steps(*steps):
-        if linked:
-            for n, stage in steps:
-                gather_step(n, stage)
-
-    T0, T1, T2, T3 = range(TILE, TILE + 4)
-    gather_steps(*((n, 0) for n in range(9)))
     x_copy.wait()
 
     def by_chunk(body):
@@ -344,15 +474,12 @@
     by_chunk(norm_one)
 
     if linked:
-        gather_steps(
-            (SLOT, 1), (KEY, 1), (SLOT, 2), (VALUE, 1), (KEY, 2), (QUERY, 1), (VALUE, 2), (OUT_W, 1), (SLOT, 3),
-            (QUERY, 2), (KEY, 3), (T0, 1), (SLOT, 4),
-        )
-        for index, core, at, odp, oslot in owners(True):
+        planned("slot")
+        for index, core, at, odp, oslot in owners(GATHER_MODES[SLOT]):
             w_slot[odp * 64 : odp * 64 + 64, oslot * 128 : oslot * 128 + 128] = ags[SLOT][core, at, 0:64, :]
         for window in range(4):
             total = jnp.zeros((16, 128), WIDE)
-            for index, core, at, _, _ in owners(True):
+            for index, core, at, _, _ in owners(GATHER_MODES[SLOT]):
                 if index // 8 == window:
                     total = total + ags[SLOT][core, at, 64:80, :].astype(WIDE)
             gains[0:8, window * 128 : window * 128 + 128] = total[0:8]
@@ -364,9 +491,9 @@
     n1[...] = low(gtwo[...] * gain_one)
     expo[...] = jnp.exp(dot(n1[...], w_slot[...]))
     proj[3] = low(expo[...])
-    gather_steps((OUT_W, 2), (VALUE, 3), (KEY, 4))
+    planned("key")
     proj[1] = low(dot(n1[...], key_w()))
-    gather_steps((T1, 1), (QUERY, 3), (VALUE, 4), (T0, 2))
+    planned("val")
     proj[2] = low(dot(n1[...], value_w()))
     def two(v):
         return jnp.concatenate([v * bd_lo[...], v * bd_hi[...]], axis=0)
@@ -389,6 +516,7 @@
             loc[0, i, p] = kw[p] * bdm[...]
             loc[1, i, p] = wv[p] * bdm[...]
 
+    planned("loc")
     by_chunk(local_states)
 
     def scan_states(order, initial, t_initial, keep):
@@ -429,11 +557,11 @@
     forward = list(range(chunks))
     takes_forward = half.astype(WIDE)
     send_states(forward, STATE)
-    gather_steps((OUT_W, 3), (T2, 1), (QUERY, 4))
+    planned("qry")
     proj[0] = low(dot(n1[...], query_w()))
     n1t[...] = n1[...].T
+    planned("scan")
     carry_states(forward, STATE, takes_forward)
-    gather_steps((OUT_W, 4), (T1, 2))
     first_half = iota2((CHUNK, LANES), 1) < 64
 
     def over_heads(lo_part, hi_part):
@@ -452,6 +580,7 @@
         )
 
     def attend(rows, i):
+        planned_at("att%d", i)
         mask = vis[i]
         carried = hcar[i]
         totals = dot(mask[:, 0:128], proj[3, rows, :]) + jnp.concatenate([carried] * PAIRS, axis=1) * tin[i, 0:1, :]
@@ -475,12 +604,10 @@
         near = [dot(mix[p], two(v[p])) for p in every]
         for p in every:
             att[rows, pair_cols[p]] = low(near[p] + carried * from_state[p])
-        if linked:
-            for at, steps in ((0, ((T0, 3),)), (1, ((T3, 1),)), (3, ((T2, 2),))):
-                pl.when(i == at)(functools.partial(gather_steps, *steps))
 
     by_chunk(attend)
 
+    planned("outp")
     mid[...] = x_v[...] + dot(att[...], out_w())
     acc[...] = mid[...]
     cot_copy.wait()
@@ -495,35 +622,28 @@
     n2t[...] = n2[...].T
     gft[...] = gf[...].T
 
-    def scatter_steps(*steps):
-        if linked:
-            for n, stage in steps:
-                scatter_step(n, stage, PIECE_ROWS[n])
+    def tile_place(t, places):
+        at = places[0]
+        for k in range(1, 4):
+            if places[k] != places[0]:
+                at = jnp.where(t == k, places[k], at)
+        return at
 
     def feed(t, _):
-        if linked:
-            for at, gathered, scattered in (
-                (0, ((T1, 3), (T0, 4)), ()),
-                (1, ((T3, 2), (T2, 3), (T1, 4)), ((T0, 1),)),
-                (2, ((T3, 3), (T2, 4)), ((T1, 1),)),
-                (3, ((T3, 4),), ((T0, 2), (T2, 1))),
-            ):
-                @pl.when(t == at)
-                def _(gathered=gathered, scattered=scattered):
-                    gather_steps(*gathered)
-                    scatter_steps(*scattered)
-
+        planned_at("ffn%da", t)
         hidden = dot(n2[...], up_w(t))
         cdf = 0.5 * (1.0 + lax.erf(hidden * 0.7071067811865476))
         active = low(hidden * cdf)
         slope = cdf + hidden * (jnp.exp(-0.5 * hidden * hidden) * 0.3989422804014327)
         grad_hidden = low(dot(gf[...], down_w(t)) * slope)
+        planned_at("ffn%db", t)
         acc[...] += dot_nt(active, down_w(t))
         gtwo[...] += dot_nt(grad_hidden, up_w(t))
         g_up = low(dot(n2t[...], grad_hidden))
         g_down = low(dot(gft[...], active))
         if linked:
-            for _, core, at, odp, oslot in owners(False):
+            for (_, core, at, odp, oslot), *later in zip(*(owners(mode) for mode in SCATTER_MODES[TILE:])):
+                at = tile_place(t, [at] + [other[2] for other in later])
                 rows, cols = slice(odp * 64, odp * 64 + 64), slice(oslot * 128, oslot * 128 + 128)
                 rss[TILE][t, core, at, 0:64, :] = g_up[rows, cols]
                 rss[TILE][t, core, at, 64:128, :] = g_down[rows, cols]
@@ -535,10 +655,6 @@
 
     lax.fori_loop(0, 4, feed, 0)
 
-    mine, theirs = out_ref.at[row, own_rows], out_ref.at[1 - row, own_rows]
-    oy, oc, of = remote(outb, mine, OUT, y_peer), remote(outb, mine, OUT + 1, partner), remote(theirs, theirs, OUT + 2, partner)
-    ol = pltpu.make_async_copy(outb, mine, lsem.at[2])
-
     def norm_two_back(rows, i):
         outb[rows, :] = low(acc[rows, :])
         xhat, inv = norm_parts(mid[rows, :])
@@ -548,18 +664,19 @@
         gf[rows, :] = low(grad)
         gains[3:4, :] = gains[3:4, :] + jnp.sum(up * xhat, axis=0, keepdims=True)
 
-    scatter_steps((T3, 1))
+    planned("n2b")
     gains[2:8, :] = jnp.zeros((6, WIDTH), WIDE)
     by_chunk(norm_two_back)
     oy.start()
     oc.start()
     ol.start()
-    scatter_steps((T0, 3))
+    planned("ga")
     ga[...] = low(dot_nt(gf[...], out_w()))
+    planned("gout")
     g_out = low(dot_tn(att[...], gf[...]))
 
     def pack_square(n, grad):
-        for index, core, at, _, _ in owners(False):
+        for index, core, at, _, _ in owners(SCATTER_MODES[n]):
             for t in range(4):
                 rss[n][core, at, t * 16 : t * 16 + 16, :] = grad[
                     index * 16 : index * 16 + 16, t * 128 : t * 128 + 128
@@ -567,11 +684,11 @@
 
     if linked:
         pack_square(OUT_W, g_out)
-        scatter_steps((OUT_W, 0))
     else:
         outs[5][...] = g_out
 
     def back_first(rows, i):
+        planned_at("B1_%d", i)
         mask = vis[i]
         carried = hcar[i]
         carried_n = hcar_n[i]
@@ -606,26 +723,41 @@
             ),
             (8, WIDTH),
         )
-        if linked:
-            for at, steps in ((0, ((OUT_W, 1),)), (1, ((T1, 2),)), (3, ((T0, 4),))):
-                pl.when(i == at)(functools.partial(scatter_steps, *steps))
+
     by_chunk(back_first)
+    planned("send2")
     sent(exchange(STATE))
     send_states(forward[::-1], BACK)
+    planned("qg")
     grad = low(dot(n1t[...], gproj[0]))
     if linked:
         pack_square(QUERY, grad)
-        scatter_steps((QUERY, 0))
     else:
         outs[2][...] = grad
+    planned("scan2")
     carry_states(forward[::-1], BACK, 1.0 - takes_forward)
-    def spread_gin(i):
-        part = pl.ds(pl.multiple_of(half * tokens + i * CHUNK, CHUNK), CHUNK)
-        mine, theirs, at = gin_ref.at[row, part], gin_ref.at[1 - row, part], GIN + 3 * i
-        source = ginb.at[pl.ds(pl.multiple_of(i * CHUNK, CHUNK), CHUNK)]
-        return remote(source, mine, at, y_peer), remote(source, mine, at + 1, partner), remote(theirs, theirs, at + 2, partner)
+    def back_value(rows, i):
+        planned_at("bv%d", i)
+        mask = vist[i]
+        ends = tail[i]
+        w, g, sc = ([m[rows, cols] for cols in pair_cols] for m in (proj.at[3], ga, scaled))
+        g2, sc2 = ([two(m[p]) for p in every] for m in (g, sc))
+        mix = [low(dot_nt(w[p], sc2[p])) * mask for p in every]
+        from_state = [dot_nt(w[p], sin[1, i, p]) for p in every]
+        near = [dot(mix[p], g2[p]) for p in every]
+        for p in every:
+            gproj[2, rows, pair_cols[p]] = low(near[p] + ends * from_state[p])
+
+    by_chunk(back_value)
+    planned("wV")
+    grad = low(dot(n1t[...], gproj[2]))
+    if linked:
+        pack_square(VALUE, grad)
+    else:
+        outs[4][...] = grad
 
     def back_second(rows, i):
+        planned_at("B2_%d", i)
         mask = vist[i]
         ends = tail[i]
         wc = dot(mask[:, 0:128], gtot[rows, :]) + jnp.concatenate([ends] * PAIRS, axis=1) * tin[i, 0:1, :]
@@ -633,14 +765,9 @@
         g, sc, gn = ([ref[rows, cols] for cols in pair_cols] for ref in (ga, scaled, gnum))
         g2, sc2, gn2, q2 = ([two(m[p]) for p in every] for m in (g, sc, gn, q))
         s_query, s_grad = ([sin[n, i, p] for p in every] for n in range(2))
-        mix = [low(dot_nt(w[p], sc2[p])) * mask for p in every]
         gmix = [low(dot_nt(v[p], g2[p])) * mask for p in every]
         cross = [low(dot_nt(k[p], q2[p])) * mask for p in every]
         gcross = [low(dot_nt(w[p], gn2[p])) * mask for p in every]
-        from_state = [dot_nt(w[p], s_grad[p]) for p in every]
-        near = [dot(mix[p], g2[p]) for p in every]
-        for p in every:
-            gproj[2, rows, pair_cols[p]] = low(near[p] + ends * from_state[p])
         from_state = [dot_nt(w[p], s_query[p]) for p in every]
         near = [dot(gcross[p], q2[p]) for p in every]
         for p in every:
@@ -655,26 +782,13 @@
         xhat, inv = norm_parts(x_v[rows, :])
         ginb[rows, :] = low(cot_v[rows, :] + norm_back(xhat, inv, gain_one, up))
         gains[2:3, :] = gains[2:3, :] + jnp.sum(up * xhat, axis=0, keepdims=True)
-        if linked:
-            for at, steps in (
-                (0, ((QUERY, 1), (T2, 2), (T1, 3))), (2, ((T3, 2),)), (3, ((OUT_W, 2), (T2, 3)))
-            ):
-                pl.when(i == at)(functools.partial(scatter_steps, *steps))
-        iy, ic = spread_gin(i)[:2]
-        iy.start()
-        ic.start()
-
-        @pl.when(i == 1)
-        def _():
-            oy.wait_recv()
-            of.start()
-
 
     by_chunk(back_second)
 
     il = pltpu.make_async_copy(ginb, gin_ref.at[row, own_rows], lsem.at[3])
     il.start()
-    for n, piece in ((2, VALUE), (1, KEY), (3, SLOT)):
+    planned("wK")
+    for n, piece in ((1, KEY), (3, SLOT)):
         grad = low(dot(n1t[...], gproj[n]))
         if n == 3:
             grad = low(dot_nt(grad, perm[...]))
@@ -683,7 +797,7 @@
         elif n < 3:
             pack_square(piece, grad)
         else:
-            for index, core, at, odp, oslot in owners(False):
+            for index, core, at, odp, oslot in owners(SCATTER_MODES[SLOT]):
                 rss[SLOT][core, at, 0:64, :] = grad[odp * 64 : odp * 64 + 64, oslot * 128 : oslot * 128 + 128]
                 window = index // 8
                 rss[SLOT][core, at, 64:80, :] = low(
@@ -691,23 +805,7 @@
                         [gains[2:4, window * 128 : window * 128 + 128], jnp.zeros((14, 128), WIDE)], axis=0
                     )
                 )
-        scatter_steps((piece, 0))
-    def forward_gin(i):
-        _, _, if_ = spread_gin(i)
-        spread_gin(i)[0].wait_recv()
-        if_.start()
-
-    scatter_steps((T1, 4), (QUERY, 2), (VALUE, 1))
-    forward_gin(0)
-    scatter_steps((KEY, 1), (T2, 4))
-    forward_gin(1)
-    scatter_steps((SLOT, 1), (T3, 3), (OUT_W, 3))
-    forward_gin(2)
-    scatter_steps((VALUE, 2), (KEY, 2))
-    forward_gin(3)
-    scatter_steps((SLOT, 2), (T3, 4), (OUT_W, 4), (QUERY, 3), (VALUE, 3), (KEY, 3))
-    scatter_steps((QUERY, 4), (SLOT, 3), (VALUE, 4), (KEY, 4))
-    scatter_steps((SLOT, 4))
+        planned("wS" if n == 1 else "end")
     if not linked:
         outs[9][...] = gains[2:4, :]
 
@@ -717,16 +815,13 @@
     of.wait()
     il.wait()
     for i in range(chunks):
-        iy, ic, if_ = spread_gin(i)
-        iy.wait_send()
-        ic.wait()
-        if_.wait()
+        spread_gin(i)[0].wait_send()
+    spread_gin_all(0).wait()
+    spread_gin_all(1).wait()
     sent(exchange(BACK))
     if linked:
         for n in range(9):
-            sent(gather_z(n) + gather_b(n) + gather_a(n) + gather_last(n))
-            for stage in range(4):
-                sent(scatter_copies(n, stage))
+            sent([scatter_all(n, stage) for stage in range(4)])
 
 
 def finish_kernel(out_ref, gin_ref, small_ref, o, g, gq, gk, gv, go, gs, gu, gd, g1, g2):
@@ -804,12 +899,16 @@
         vm((CHUNK, LANES), NARROW), vm((CHUNK, LANES), NARROW), vm((CHUNK, LANES), WIDE),
         vm((2, PAIRS, 128, 128), WIDE), vm((2, 2, PAIRS, 128, 128), WIDE),
         vm((8, width), WIDE), vm((2, 8, width), WIDE),
-        pltpu.SemaphoreType.DMA((152,)), pltpu.SemaphoreType.DMA((152,)), pltpu.SemaphoreType.DMA((12,)),
+        pltpu.SemaphoreType.DMA((88,)), pltpu.SemaphoreType.DMA((88,)), pltpu.SemaphoreType.DMA((12,)),
     ]
     if linked:
-        for lead in ((2, 16), (2, 16), (16,), (8,), (4,), (3,)):
+        for lead in ((2, 16), (2, 16), (16,)):
             scratch += [vm((*lead, r, LANES), NARROW) for r in PIECE_ROWS[:TILE]]
             scratch += [vm((4, *lead, 128, LANES), NARROW)]
+        for k in range(3):
+            for r, mode in zip(PIECE_ROWS, SCATTER_MODES):
+                sizes, steps = strides(mode)
+                scratch += [vm(((sizes[k] - 1) * steps[k], r, LANES), NARROW)]
     else:
         scratch += [vm((4, width, width), NARROW)] * 3
     anywhere = pl.BlockSpec(memory_space=pl.ANY)

time: 111 us -> 99.1 us (0.89)
  Pallas kernels: 110 us -> 98.2 us
    pallas_call x1, Pallas kernels: 104 us -> 91.8 us  [run_block(): pl.pallas_call(functools.partial(block_kernel, linked, 12, 2 + len(small)...]
where the time goes in v3:
time: 99.1 us; the launch traced here: 98.8 us
  Pallas kernels  98.2 us (99%)
    pallas_call x1, Pallas kernels, run_block(): pl.pallas_call(functools.partial(block_kernel, linked, 12, 2 + len(small)...  91.8 us
    pallas_call x1, Pallas kernels, finish(): pl.pallas_call(finish_kernel, grid=(rows * length // 512,), out_shape=[sh...  6.33 us

profile of v3, /device:TPU:0, one launch (start us, length us, event | category | flops | bytes accessed | tf_op | source)
XLA Modules:
  0.0 98.8 jit_solution(11655394133863004117)
XLA Ops:
  0.6 91.8 %shard_map.203 = (bf16[2,1024,512]{2,1,0:T(8,128)(2,1)}, bf16[2,1024,512]{2,1,0:T(8,128)(2,1)}, f32[848,128]{1,0:T(8,128)}) custom-call(f32[2,1024,512]{2,1,0:T(8,128)} %refs_0_.1, s32[2,1024]{1,0:T(2,128)} %refs_1_.1, f32[2,1024,512]{2,1,0:T(8,128)} %refs_2_.1, bf16[16,512]{1,0:T(8,128)(2,1)} %refs_3_.1, bf16[16,512]{1,0:T(8,128)(2,1)} %refs_4_.1, ...), custom_call_target="tpu_custom_call" | custom-call | tf_op jit(solution)/shard_map/pallas_call | solution.py:925
  92.5 6.3 %shard_map.204 = (f32[2,1024,512]{2,1,0:T(8,128)}, f32[2,1024,512]{2,1,0:T(8,128)}, f32[16,512]{1,0:T(8,128)}, f32[16,512]{1,0:T(8,128)}, f32[16,512]{1,0:T(8,12...) custom-call(bf16[2,1024,512]{2,1,0:T(8,128)(2,1)} %get-tuple-element, ...), custom_call_target="tpu_custom_call" | custom-call | tf_op jit(solution)/shard_map/pallas_call | solution.py:866

commit v4 on v3

--- a/solution.py
+++ b/solution.py
@@ -21,43 +21,43 @@
 SLOT, KEY, VALUE, QUERY, OUT_W, TILE = range(6)
 SMALL_ROWS = sum(PIECE_ROWS)
 GATHER_MODES = (
-    ("ABZ", "m"), ("ABZ", "m"), ("ABZ", "m"), ("ABZ", "m"), ("ABZ", "m"),
+    ("PZ", "y"), ("PZ", "x"), ("PZ", "y"), ("PZ", "y"), ("ZAB", "y"),
     ("ABZ", "m"), ("ABZ", "m"), ("ABZ", "m"), ("ABZ", "m"),
 )
 SCATTER_MODES = (
-    ("ABZ", "x"), ("ABZ", "m"), ("ABZ", "x"), ("AZB", "x"), ("ABZ", "m"),
-    ("ABZ", "m"), ("AZB", "m"), ("AZB", "x"), ("ABZ", "x"),
+    ("PZ", "x"), ("AZB", "x"), ("PZ", "x"), ("AZB", "x"), ("AZB", "x"),
+    ("PZ", "y"), ("ZAB", "x"), ("AZB", "x"), ("ABZ", "x"),
 )
 PLAN = {
-    "slot": ("S1", "K1", "V1", "S2", "K2", "Q1", "V2", "O1", "S3", "K3", "T01", "Q2", "S4",),
-    "key": ("V3", "K4", "O2",),
-    "val": ("V4",),
-    "loc": ("T11", "Q3", "T02",),
-    "qry": ("Q4", "O3",),
-    "scan": ("O4", "T21",),
-    "att0": ("T12",),
-    "att3": ("T31",),
-    "outp": ("T03", "T22",),
-    "ffn0a": ("T13", "T04",),
-    "ffn0b": ("T32",),
-    "ffn1a": ("T14",),
-    "ffn1b": ("T23",),
-    "ffn2a": ("T0.1", "T24",),
-    "ffn2b": ("T33",),
+    "slot": ("O1", "S1", "K1", "V1", "Q1", "S2", "K2", "T11", "S3", "V2",),
+    "key": ("T01", "V3", "K3", "O2",),
+    "val": ("T21",),
+    "loc": ("Q2", "T12",),
+    "qry": ("Q3", "T02",),
+    "scan": ("T31",),
+    "att1": ("T13",),
+    "att2": ("T22",),
+    "att3": ("T14", "O3",),
+    "outp": ("T03", "O4", "T32",),
+    "ffn0a": ("T04",),
+    "ffn1a": ("T23",),
+    "ffn2a": ("T24",),
+    "ffn2b": ("T33", "T0.1",),
     "ffn3a": ("T1.1", "T34",),
-    "n2b": ("T0.2",),
-    "ga": ("T2.1",),
-    "gout": ("T1.2",),
-    "B1_2": ("O.0",),
-    "scan2": ("T0.3", "T3.1", "Q.0", "T2.2", "O.1",),
-    "B2_1": ("y0",),
-    "B2_2": ("V.0", "y1", "Q.1",),
-    "B2_3": ("V.1", "O.2", "T3.2",),
-    "wS": ("K.0", "Q.2",),
+    "ga": ("o2", "o1", "T2.1",),
+    "qg": ("o3", "o0", "T3.1", "O.0",),
+    "scan2": ("T0.2", "Q.0",),
+    "B2_0": ("T2.2",),
+    "B2_1": ("y0", "Q.1",),
+    "B2_2": ("y1",),
+    "B2_3": ("O.1", "V.0", "T3.2",),
+    "G3": ("T1.2",),
+    "wK": ("Q.2",),
+    "wS": ("K.0", "y3",),
     "end": (
-        "S.0", "K.1", "V.2", "O.3", "y2", "S.1", "K.2", "T3.3", "Q.3", "V.3", "S.2", "f0", "T2.3", "T0.4",
-        "T1.3", "K.3", "y3", "f", "T3.4", "f2", "V.4", "S.3", "T1.4", "T2.4", "Q.4", "K.4", "O.4", "f1",
-        "S.4", "f3",
+        "p0", "O.2", "K.1", "S.0", "T3.3", "p1", "V.1", "K.2", "S.1", "O.3", "V.2", "y2", "f3", "p2",
+        "f1", "S.2", "Q.3", "T2.3", "T3.4", "T0.3", "T1.3", "K.3", "O.4", "f2", "p3", "f0", "Q.4", "T2.4",
+        "T1.4", "V.3", "K.4", "S.3",
     ),
 }
 SEMS = 4
@@ -99,8 +99,11 @@
 
 
 def strides(mode):
-    sizes = tuple(4 if axis == "Z" else 2 for axis in mode[0])
-    return sizes, (sizes[1] * sizes[2], sizes[2], 1)
+    sizes = [2 if axis in "AB" else 4 for axis in mode[0]]
+    steps = [1]
+    for size in sizes[:0:-1]:
+        steps.insert(0, steps[0] * size)
+    return sizes, steps
 
 
 def owners(mode):
@@ -110,7 +113,7 @@
         for slot in range(4):
             z, x, y, c = dp // 2, dp % 2, slot // 2, slot % 2
             first_y = mode[1] == "y" or (mode[1] == "m" and c == 0)
-            at = {"A": y if first_y else x, "B": x if first_y else y, "Z": z}
+            at = {"A": y if first_y else x, "B": x if first_y else y, "Z": z, "P": x * 2 + y}
             place = sum(at[axis] * step for axis, step in zip(mode[0], steps))
             out.append((dp * 4 + slot, c, place, dp, slot))
     return out
@@ -173,7 +176,8 @@
             ),
         }
         z_peers = [((((z + s) % 4) * 2 + x), slot) for s in (1, 2, 3)]
-        peers = [partner, x_peer, y_peer] + z_peers
+        diagonal = (z * 2 + 1 - x, (1 - y) * 2 + c)
+        peers = [partner, x_peer, y_peer, diagonal] + z_peers
     else:
         peers = [partner, y_peer]
 
@@ -217,10 +221,11 @@
             "A": (pa, [(1 - pa, dev_a)]),
             "B": (pb, [(1 - pb, dev_b)]),
             "Z": (z, [((z + s + 1) % 4, z_peers[s]) for s in range(3)]),
+            "P": (x * 2 + y, [((1 - x) * 2 + y, x_peer), (x * 2 + 1 - y, y_peer), ((1 - x) * 2 + 1 - y, diagonal)]),
         }
         return [(known[axis][0], step, known[axis][1]) for axis, step in zip(mode[0], strides(mode)[1])]
 
-    def place_in(mode, upto=3):
+    def place_in(mode, upto=None):
         return sum(at * step for at, step, _ in axes(mode)[:upto])
 
     def gather_along(n, k):
@@ -238,8 +243,8 @@
         mode = mode_of(GATHER_MODES, n)
         _, step, others = axes(mode)[k]
         base = place_in(mode, k)
-        if k == 2:
-            parts = [pl.ds(base, strides(mode)[0][2])]
+        if k == len(mode[0]) - 1:
+            parts = [pl.ds(base, strides(mode)[0][k])]
         else:
             parts = [pl.ds(base + place * step, step) for place, _ in others]
         refs = [view(ags, n).at[c, part] for part in parts]
@@ -250,18 +255,19 @@
         return remote(every_block, every_block, n * SEMS + 3, partner)
 
     def gather_step(n, stage):
-        if stage == 4:
+        count = len(mode_of(GATHER_MODES, n)[0])
+        if stage > count:
             gather_across_all(n).wait_recv()
             return
         if stage:
-            gather_along_all(n, 3 - stage).wait_recv()
-        if stage < 3:
-            start(gather_along(n, 2 - stage))
+            gather_along_all(n, count - stage).wait_recv()
+        if stage < count:
+            start(gather_along(n, count - 1 - stage))
         if stage:
-            start(gather_across(n, 3 - stage))
+            start(gather_across(n, count - stage))
 
     def gather_sent(n):
-        sent([gather_along_all(n, k) for k in range(3)] + [gather_across_all(n)])
+        sent([gather_along_all(n, k) for k in range(len(mode_of(GATHER_MODES, n)[0]))] + [gather_across_all(n)])
 
     def scatter_copies(n, stage):
         buf, at, send = view(rss, n), SCATTER + n * SEMS + stage, n * SEMS + stage
@@ -296,7 +302,7 @@
                     total = total + got[k * count + i].astype(WIDE)
                 return total
 
-            if stage < 4:
+            if stage <= len(mode[0]):
                 def step(i, _):
                     buf[c, first + i] = low(summed(i))
                     return 0
@@ -306,12 +312,12 @@
                 small_ref[pl.ds(sum(PIECE_ROWS[:n]), rows), :] = summed(0)
         else:
             gather_sent(n)
-        if stage < 4:
+        if stage <= (len(SCATTER_MODES[n][0]) if stage else 1):
             start(scatter_copies(n, stage))
 
     SCATTER = 9 * SEMS
     STATE = SCATTER + 9 * SEMS
-    BACK, OUT, GIN = STATE + 2, STATE + 4, STATE + 7
+    BACK, OUT, GIN = STATE + 2, STATE + 4, STATE + 10
 
     ins_w = ins[3:]
     if linked:
@@ -368,43 +374,39 @@
 
     pl.semaphore_wait(barrier, len(peers))
 
-    mine, theirs = out_ref.at[row, own_rows], out_ref.at[1 - row, own_rows]
-    oy, oc, of = remote(outb, mine, OUT, y_peer), remote(outb, mine, OUT + 1, partner), remote(theirs, theirs, OUT + 2, partner)
-    ol = pltpu.make_async_copy(outb, mine, lsem.at[2])
-
-    def spread_gin(i):
+    ol = pltpu.make_async_copy(outb, out_ref.at[row, own_rows], lsem.at[2])
+    results = {OUT: (outb, out_ref), GIN: (ginb, gin_ref)}
+
+    def spread(base, i):
+        source, target = results[base]
         part = pl.ds(pl.multiple_of(half * tokens + i * CHUNK, CHUNK), CHUNK)
-        mine, theirs = gin_ref.at[row, part], gin_ref.at[1 - row, part]
-        source = ginb.at[pl.ds(pl.multiple_of(i * CHUNK, CHUNK), CHUNK)]
+        mine, theirs = target.at[row, part], target.at[1 - row, part]
+        chunk = source.at[pl.ds(i * CHUNK, CHUNK)]
         return (
-            remote(source, mine, GIN + i, y_peer),
-            remote(source, mine, GIN + chunks, partner),
-            remote(theirs, theirs, GIN + chunks + 1, partner),
+            remote(chunk, mine, base + i, y_peer),
+            remote(chunk, mine, base + chunks, partner),
+            remote(theirs, theirs, base + chunks + 1, partner),
         )
 
-    def spread_gin_all(k):
-        mine = gin_ref.at[row, own_rows]
-        return remote(mine, mine, GIN + chunks + k, partner)
+    def spread_all(base, k):
+        mine = results[base][1].at[row, own_rows]
+        return remote(mine, mine, base + chunks + k, partner)
 
     def spread_steps(word):
-        if word == "f":
-            oy.wait_recv()
-            of.start()
-            return
-        sends = spread_gin(int(word[1]))
-        if word[0] == "y":
-            sends[0].start()
-            sends[1].start()
+        copies = spread(OUT if word[0] in "op" else GIN, int(word[1]))
+        if word[0] in "oy":
+            copies[0].start()
+            copies[1].start()
         else:
-            sends[0].wait_recv()
-            sends[2].start()
+            copies[0].wait_recv()
+            copies[2].start()
 
     names = {"S": SLOT, "K": KEY, "V": VALUE, "Q": QUERY, "O": OUT_W}
     names.update({"T%d" % t: TILE + t for t in range(4)})
 
     def planned(block):
         for word in PLAN.get(block, ()):
-            if word[0] in "yf":
+            if word[0] in "opyf":
                 spread_steps(word)
             elif linked:
                 if "." in word:
@@ -667,8 +669,6 @@
     planned("n2b")
     gains[2:8, :] = jnp.zeros((6, WIDTH), WIDE)
     by_chunk(norm_two_back)
-    oy.start()
-    oc.start()
     ol.start()
     planned("ga")
     ga[...] = low(dot_nt(gf[...], out_w()))
@@ -777,6 +777,7 @@
         for p in every:
             gw = low(near[p] + ends * from_state[p] + wc[:, pair_cols[p]]).astype(WIDE)
             gproj[3, rows, pair_cols[p]] = low(gw * expo[rows, pair_cols[p]])
+        planned_at("G%d", i)
         up = dot_nt(gproj[0, rows, :], query_w()) + dot_nt(gproj[1, rows, :], key_w())
         up = up + dot_nt(gproj[2, rows, :], value_w()) + dot_nt(gproj[3, rows, :], w_slot[...])
         xhat, inv = norm_parts(x_v[rows, :])
@@ -809,24 +810,25 @@
     if not linked:
         outs[9][...] = gains[2:4, :]
 
-    oc.wait()
-    oy.wait_send()
     ol.wait()
-    of.wait()
     il.wait()
-    for i in range(chunks):
-        spread_gin(i)[0].wait_send()
-    spread_gin_all(0).wait()
-    spread_gin_all(1).wait()
+    for base in (OUT, GIN):
+        for i in range(chunks):
+            spread(base, i)[0].wait_send()
+        spread_all(base, 0).wait()
+        spread_all(base, 1).wait()
     sent(exchange(BACK))
     if linked:
         for n in range(9):
-            sent([scatter_all(n, stage) for stage in range(4)])
+            sent([scatter_all(n, stage) for stage in range(len(SCATTER_MODES[n][0]) + 1)])
 
 
 def finish_kernel(out_ref, gin_ref, small_ref, o, g, gq, gk, gv, go, gs, gu, gd, g1, g2):
-    o[...] = out_ref[...].astype(WIDE)
-    g[...] = gin_ref[...].astype(WIDE)
+    step = pl.program_id(0)
+    per_row = out_ref.shape[1] // o.shape[1]
+    rows = pl.ds(pl.multiple_of((step % per_row) * o.shape[1], o.shape[1]), o.shape[1])
+    o[0] = out_ref[step // per_row, rows, :].astype(WIDE)
+    g[0] = gin_ref[step // per_row, rows, :].astype(WIDE)
 
     @pl.when(pl.program_id(0) == 0)
     def _():
@@ -859,18 +861,20 @@
 
 def finish(out, gin, small):
     rows, length, width = out.shape
-    block = pl.BlockSpec((1, 512, width), lambda i: (i // (length // 512), i % (length // 512), 0))
+    count = 512
+    block = pl.BlockSpec((1, count, width), lambda i: (i // (length // count), i % (length // count), 0))
+    here = pl.BlockSpec(memory_space=pltpu.VMEM)
     whole = lambda shape: pl.BlockSpec(shape, lambda i: (0,) * len(shape))
     shapes = [(16, width)] * 4 + [(64, 128), (64, width), (64, width), (1, 16), (1, 16)]
     shape = jax.ShapeDtypeStruct
     return pl.pallas_call(
         finish_kernel,
-        grid=(rows * length // 512,),
+        grid=(rows * length // count,),
         out_shape=[shape(out.shape, WIDE)] * 2 + [shape(s, WIDE) for s in shapes],
-        in_specs=[block, block, whole(small.shape)],
+        in_specs=[here] * 3,
         out_specs=[block, block] + [whole(s) for s in shapes],
-        compiler_params=pltpu.CompilerParams(vmem_limit_bytes=60 * 1024 * 1024),
-    )(out, gin, small)
+        compiler_params=pltpu.CompilerParams(vmem_limit_bytes=32 * 1024 * 1024),
+    )(*(pltpu.with_memory_space_constraint(v, pltpu.VMEM) for v in (out, gin, small)))
 
 
 def run_block(linked, inputs, starts, cotangent, weights):
@@ -908,16 +912,17 @@
         for k in range(3):
             for r, mode in zip(PIECE_ROWS, SCATTER_MODES):
                 sizes, steps = strides(mode)
-                scratch += [vm(((sizes[k] - 1) * steps[k], r, LANES), NARROW)]
+                blocks = (sizes[k] - 1) * steps[k] if k < len(sizes) else 0
+                scratch += [vm((blocks, r, LANES) if blocks else (1, 16, LANES), NARROW)]
     else:
         scratch += [vm((4, width, width), NARROW)] * 3
     anywhere = pl.BlockSpec(memory_space=pl.ANY)
     here = pl.BlockSpec(memory_space=pltpu.VMEM)
     shape = jax.ShapeDtypeStruct
-    big = [shape((rows, length, width), NARROW)] * 2
+    big = [pltpu.VMEM((rows, length, width), NARROW)] * 2
     square = (width, width)
     if linked:
-        small = [shape((SMALL_ROWS, LANES), WIDE)]
+        small = [pltpu.VMEM((SMALL_ROWS, LANES), WIDE)]
         weight_specs = [here] * 9
     else:
         small = [shape(square, NARROW)] * 5 + [shape((4, *square), NARROW)] * 2 + [shape((2, width), WIDE)]
@@ -926,10 +931,10 @@
         functools.partial(block_kernel, linked, 12, 2 + len(small)),
         out_shape=big + small,
         in_specs=[anywhere, here, anywhere] + weight_specs,
-        out_specs=[anywhere] * 2 + [here] * len(small),
+        out_specs=[here] * (2 + len(small)),
         scratch_shapes=scratch,
         compiler_params=pltpu.CompilerParams(
-            collective_id=0, has_side_effects=True, vmem_limit_bytes=62 * 1024 * 1024
+            collective_id=0, has_side_effects=True, vmem_limit_bytes=57 * 1024 * 1024
         ),
     )(inputs, starts, cotangent, *weights)
 

time: 99.1 us -> 92.1 us (0.929)
  Pallas kernels: 98.2 us -> 91.2 us
    pallas_call x1, Pallas kernels: 91.8 us -> 87.4 us  [run_block(): pl.pallas_call(functools.partial(block_kernel, linked, 12, 2 + len(small)...]
    pallas_call x1, Pallas kernels: 6.33 us -> 3.85 us  [finish(): pl.pallas_call(finish_kernel, grid=(rows * length // count,), out_shape=[...]
where the time goes in v4:
time: 92.1 us; the launch traced here: 91.9 us
  Pallas kernels  91.2 us (99%)
    pallas_call x1, Pallas kernels, run_block(): pl.pallas_call(functools.partial(block_kernel, linked, 12, 2 + len(small)...  87.4 us
    pallas_call x1, Pallas kernels, finish(): pl.pallas_call(finish_kernel, grid=(rows * length // count,), out_shape=[...  3.85 us

profile of v4, /device:TPU:0, one launch (start us, length us, event | category | flops | bytes accessed | tf_op | source)
XLA Modules:
  0.0 91.9 jit_solution(4984262803045284702)
XLA Ops:
  0.6 87.4 %shard_map.203 = (bf16[2,1024,512]{2,1,0:T(8,128)(2,1)S(1)}, bf16[2,1024,512]{2,1,0:T(8,128)(2,1)S(1)}, f32[848,128]{1,0:T(8,128)S(1)}) custom-call(f32[2,1024,512]{2,1,0:T(8,128)} %refs_0_.1, s32[2,1024]{1,0:T(2,128)} %refs_1_.1, f32[2,1024,512]{2,1,0:T(8,128)} %refs_2_.1, bf16[16,512]{1,0:T(8,128)(2,1)} %refs_3_.1, bf16[16,512]{1,0:T(8,128)(2,1)} %refs_4_.1, ...), custom_call_target="tpu_custom_call" | custom-call | tf_op jit(solution)/shard_map/pallas_call | solution.py:930
  88.0 3.9 %shard_map.204 = (f32[2,1024,512]{2,1,0:T(8,128)}, f32[2,1024,512]{2,1,0:T(8,128)}, f32[16,512]{1,0:T(8,128)}, f32[16,512]{1,0:T(8,128)}, f32[16,512]{1,0:T(8,12...) custom-call(bf16[2,1024,512]{2,1,0:T(8,128)(2,1)S(1)} %get-tuple-ele, ...), custom_call_target="tpu_custom_call" | custom-call | tf_op jit(solution)/shard_map/pallas_call | solution.py:870

commit v5 on v4

--- a/solution.py
+++ b/solution.py
@@ -21,43 +21,43 @@
 SLOT, KEY, VALUE, QUERY, OUT_W, TILE = range(6)
 SMALL_ROWS = sum(PIECE_ROWS)
 GATHER_MODES = (
-    ("PZ", "y"), ("PZ", "x"), ("PZ", "y"), ("PZ", "y"), ("ZAB", "y"),
-    ("ABZ", "m"), ("ABZ", "m"), ("ABZ", "m"), ("ABZ", "m"),
+    ("ABZ", "m"), ("ABZ", "m"), ("ABZ", "m"), ("ABZ", "m"), ("ABZ", "m"),
+    ("ABZ", "m"), ("AZB", "m"), ("ABZ", "m"), ("AZB", "m"),
 )
 SCATTER_MODES = (
-    ("PZ", "x"), ("AZB", "x"), ("PZ", "x"), ("AZB", "x"), ("AZB", "x"),
-    ("PZ", "y"), ("ZAB", "x"), ("AZB", "x"), ("ABZ", "x"),
+    ("ABZ", "m"), ("AZB", "x"), ("ABZ", "x"), ("ABZ", "m"), ("ABZ", "m"),
+    ("ABZ", "y"), ("ZAB", "x"), ("AZB", "x"), ("AZB", "x"),
 )
 PLAN = {
-    "slot": ("O1", "S1", "K1", "V1", "Q1", "S2", "K2", "T11", "S3", "V2",),
-    "key": ("T01", "V3", "K3", "O2",),
-    "val": ("T21",),
-    "loc": ("Q2", "T12",),
-    "qry": ("Q3", "T02",),
-    "scan": ("T31",),
-    "att1": ("T13",),
-    "att2": ("T22",),
-    "att3": ("T14", "O3",),
-    "outp": ("T03", "O4", "T32",),
-    "ffn0a": ("T04",),
-    "ffn1a": ("T23",),
+    "slot": (
+        "S1", "K1", "T11", "V1", "S2", "Q1", "K2", "V2", "S3", "O1", "T01", "K3", "S4", "Q2",
+        "V3", "K4", "T31", "T21",
+    ),
+    "val": ("O2", "V4", "T02",),
+    "qry": ("Q3", "Q4", "T12",),
+    "att0": ("O3",),
+    "att1": ("T22",),
+    "att3": ("T03",),
+    "outp": ("O4",),
+    "ffn0a": ("T04", "T32", "T13",),
+    "ffn1a": ("T23", "T14",),
     "ffn2a": ("T24",),
     "ffn2b": ("T33", "T0.1",),
     "ffn3a": ("T1.1", "T34",),
-    "ga": ("o2", "o1", "T2.1",),
-    "qg": ("o3", "o0", "T3.1", "O.0",),
-    "scan2": ("T0.2", "Q.0",),
-    "B2_0": ("T2.2",),
-    "B2_1": ("y0", "Q.1",),
-    "B2_2": ("y1",),
-    "B2_3": ("O.1", "V.0", "T3.2",),
-    "G3": ("T1.2",),
-    "wK": ("Q.2",),
-    "wS": ("K.0", "y3",),
+    "ga": ("o1", "T2.1", "o0",),
+    "B1_1": ("O.0", "T3.1",),
+    "send2": ("o2",),
+    "qg": ("o3", "p1",),
+    "scan2": ("Q.0", "T2.2", "O.1",),
+    "B2_0": ("V.0",),
+    "B2_1": ("Q.1", "T0.2",),
+    "B2_2": ("T3.2", "y1",),
+    "B2_3": ("y2", "V.1",),
+    "wS": ("O.2", "K.0",),
     "end": (
-        "p0", "O.2", "K.1", "S.0", "T3.3", "p1", "V.1", "K.2", "S.1", "O.3", "V.2", "y2", "f3", "p2",
-        "f1", "S.2", "Q.3", "T2.3", "T3.4", "T0.3", "T1.3", "K.3", "O.4", "f2", "p3", "f0", "Q.4", "T2.4",
-        "T1.4", "V.3", "K.4", "S.3",
+        "S.0", "p3", "Q.2", "T2.3", "T0.3", "K.1", "S.1", "V.2", "O.3", "Q.3", "T1.2", "y0", "K.2", "T3.3",
+        "S.2", "T2.4", "V.3", "p0", "y3", "O.4", "f0", "p2", "S.3", "T1.3", "T3.4", "T0.4", "f2", "f1",
+        "K.3", "f3", "V.4", "Q.4", "T1.4", "K.4", "S.4",
     ),
 }
 SEMS = 4
@@ -129,12 +129,23 @@
     )
 
 
+def tile_place(t, places):
+    at = places[0]
+    for k in range(1, 4):
+        if places[k] != places[0]:
+            at = jnp.where(t == k, places[k], at)
+    return at
+
+
 def tile_of(buf, n, first):
-    place = {(dp, slot): (core, at) for _, core, at, dp, slot in owners(GATHER_MODES[TILE])}
+    spots = {}
+    for each in zip(*(owners(mode) for mode in GATHER_MODES[TILE:])):
+        _, core, _, dp, slot = each[0]
+        spots[dp, slot] = core, tile_place(n, [at for _, _, at, _, _ in each])
     return jnp.concatenate(
         [
             jnp.concatenate(
-                [buf[(n, *place[dp, slot], slice(first, first + 64), slice(None))] for dp in range(8)], axis=0
+                [buf[(n, *spots[dp, slot], slice(first, first + 64), slice(None))] for dp in range(8)], axis=0
             )
             for slot in range(4)
         ],
@@ -177,7 +188,7 @@
         }
         z_peers = [((((z + s) % 4) * 2 + x), slot) for s in (1, 2, 3)]
         diagonal = (z * 2 + 1 - x, (1 - y) * 2 + c)
-        peers = [partner, x_peer, y_peer, diagonal] + z_peers
+        peers = [partner, x_peer, y_peer] + z_peers
     else:
         peers = [partner, y_peer]
 
@@ -193,7 +204,8 @@
 
     def remote(src, dst, at, device, send_at=None):
         return pltpu.make_async_remote_copy(
-            src_ref=src, dst_ref=dst, send_sem=ssem.at[at if send_at is None else send_at], recv_sem=rsem.at[at],
+            src_ref=src, dst_ref=dst, recv_sem=rsem.at[at],
+            send_sem=ssem.at[send_at if send_at is not None else at if at < SCATTER else at - SCATTER],
             device_id=device, device_id_type=MESH,
         )
 
@@ -210,10 +222,7 @@
             copy.wait_send()
 
     def view(bufs, n):
-        return bufs[n] if isinstance(n, int) and n < TILE else bufs[TILE].at[n - TILE]
-
-    def mode_of(modes, n):
-        return modes[n if isinstance(n, int) else TILE]
+        return bufs[n] if n < TILE else bufs[TILE].at[n - TILE]
 
     def axes(mode):
         pa, pb, dev_a, dev_b = near[mode[1]]
@@ -229,18 +238,18 @@
         return sum(at * step for at, step, _ in axes(mode)[:upto])
 
     def gather_along(n, k):
-        mode = mode_of(GATHER_MODES, n)
+        mode = GATHER_MODES[n]
         _, step, others = axes(mode)[k]
         part = view(ags, n).at[c, pl.ds(place_in(mode, k + 1), step)]
         return [remote(part, part, n * SEMS + k, device) for _, device in others]
 
     def gather_along_all(n, k):
-        _, step, others = axes(mode_of(GATHER_MODES, n))[k]
+        _, step, others = axes(GATHER_MODES[n])[k]
         part = view(ags, n).at[c, pl.ds(0, step * len(others))]
         return remote(part, part, n * SEMS + k, partner)
 
     def gather_across(n, k):
-        mode = mode_of(GATHER_MODES, n)
+        mode = GATHER_MODES[n]
         _, step, others = axes(mode)[k]
         base = place_in(mode, k)
         if k == len(mode[0]) - 1:
@@ -255,7 +264,7 @@
         return remote(every_block, every_block, n * SEMS + 3, partner)
 
     def gather_step(n, stage):
-        count = len(mode_of(GATHER_MODES, n)[0])
+        count = len(GATHER_MODES[n][0])
         if stage > count:
             gather_across_all(n).wait_recv()
             return
@@ -267,7 +276,7 @@
             start(gather_across(n, count - stage))
 
     def gather_sent(n):
-        sent([gather_along_all(n, k) for k in range(len(mode_of(GATHER_MODES, n)[0]))] + [gather_across_all(n)])
+        sent([gather_along_all(n, k) for k in range(len(GATHER_MODES[n][0]))] + [gather_across_all(n)])
 
     def scatter_copies(n, stage):
         buf, at, send = view(rss, n), SCATTER + n * SEMS + stage, n * SEMS + stage
@@ -338,8 +347,8 @@
         spread = jnp.where(iota2((16, 128), 1) == iota2((16, 128), 0) + lane_at, 1.0, 0.0)
         ags[SLOT][c, place[SLOT], pl.ds(64, 16), :] = low(dot(low(both), low(spread)))
         for t in range(4):
-            ags[TILE][t, c, place[TILE], pl.ds(0, 64), :] = wu[:, t * 128 : t * 128 + 128]
-            ags[TILE][t, c, place[TILE], pl.ds(64, 64), :] = wd[:, t * 128 : t * 128 + 128]
+            ags[TILE][t, c, place[TILE + t], pl.ds(0, 64), :] = wu[:, t * 128 : t * 128 + 128]
+            ags[TILE][t, c, place[TILE + t], pl.ds(64, 64), :] = wd[:, t * 128 : t * 128 + 128]
         query_w, key_w, value_w, out_w = (
             functools.partial(square_of, ags[n], n) for n in (QUERY, KEY, VALUE, OUT_W)
         )
@@ -624,13 +633,6 @@
     n2t[...] = n2[...].T
     gft[...] = gf[...].T
 
-    def tile_place(t, places):
-        at = places[0]
-        for k in range(1, 4):
-            if places[k] != places[0]:
-                at = jnp.where(t == k, places[k], at)
-        return at
-
     def feed(t, _):
         planned_at("ffn%da", t)
         hidden = dot(n2[...], up_w(t))
@@ -649,7 +651,8 @@
                 rows, cols = slice(odp * 64, odp * 64 + 64), slice(oslot * 128, oslot * 128 + 128)
                 rss[TILE][t, core, at, 0:64, :] = g_up[rows, cols]
                 rss[TILE][t, core, at, 64:128, :] = g_down[rows, cols]
-            scatter_step(TILE + t, 0, 128)
+            for k in range(4):
+                pl.when(t == k)(functools.partial(scatter_step, TILE + k, 0, 128))
         else:
             outs[7][t] = g_up
             outs[8][t] = g_down
@@ -903,7 +906,7 @@
         vm((CHUNK, LANES), NARROW), vm((CHUNK, LANES), NARROW), vm((CHUNK, LANES), WIDE),
         vm((2, PAIRS, 128, 128), WIDE), vm((2, 2, PAIRS, 128, 128), WIDE),
         vm((8, width), WIDE), vm((2, 8, width), WIDE),
-        pltpu.SemaphoreType.DMA((88,)), pltpu.SemaphoreType.DMA((88,)), pltpu.SemaphoreType.DMA((12,)),
+        pltpu.SemaphoreType.DMA((52,)), pltpu.SemaphoreType.DMA((88,)), pltpu.SemaphoreType.DMA((4 if linked else 12,)),
     ]
     if linked:
         for lead in ((2, 16), (2, 16), (16,)):

time: 92.1 us -> 89.5 us (0.972)
  Pallas kernels: 91.2 us -> 88.6 us
    pallas_call x1, Pallas kernels: 87.4 us -> 84.7 us  [run_block(): pl.pallas_call(functools.partial(block_kernel, linked, 12, 2 + len(small)...]
where the time goes in v5:
time: 89.5 us; the launch traced here: 89.3 us
  Pallas kernels  88.6 us (99%)
    pallas_call x1, Pallas kernels, run_block(): pl.pallas_call(functools.partial(block_kernel, linked, 12, 2 + len(small)...  84.7 us
    pallas_call x1, Pallas kernels, finish(): pl.pallas_call(finish_kernel, grid=(rows * length // count,), out_shape=[...  3.85 us

profile of v5, /device:TPU:0, one launch (start us, length us, event | category | flops | bytes accessed | tf_op | source)
XLA Modules:
  0.0 89.3 jit_solution(12380720564537404803)
XLA Ops:
  0.6 84.7 %shard_map.203 = (bf16[2,1024,512]{2,1,0:T(8,128)(2,1)S(1)}, bf16[2,1024,512]{2,1,0:T(8,128)(2,1)S(1)}, f32[848,128]{1,0:T(8,128)S(1)}) custom-call(f32[2,1024,512]{2,1,0:T(8,128)} %refs_0_.1, s32[2,1024]{1,0:T(2,128)} %refs_1_.1, f32[2,1024,512]{2,1,0:T(8,128)} %refs_2_.1, bf16[16,512]{1,0:T(8,128)(2,1)} %refs_3_.1, bf16[16,512]{1,0:T(8,128)(2,1)} %refs_4_.1, ...), custom_call_target="tpu_custom_call" | custom-call | tf_op jit(solution)/shard_map/pallas_call | solution.py:933
  85.4 3.9 %shard_map.204 = (f32[2,1024,512]{2,1,0:T(8,128)}, f32[2,1024,512]{2,1,0:T(8,128)}, f32[16,512]{1,0:T(8,128)}, f32[16,512]{1,0:T(8,128)}, f32[16,512]{1,0:T(8,12...) custom-call(bf16[2,1024,512]{2,1,0:T(8,128)(2,1)S(1)} %get-tuple-ele, ...), custom_call_target="tpu_custom_call" | custom-call | tf_op jit(solution)/shard_map/pallas_call | solution.py:873

commit v6 on v5

--- a/solution.py
+++ b/solution.py
@@ -60,6 +60,7 @@
         "K.3", "f3", "V.4", "Q.4", "T1.4", "K.4", "S.4",
     ),
 }
+Z_ORDER = (2, 1, 3)
 SEMS = 4
 
 
@@ -186,7 +187,7 @@
                 (z * 2 + x + (1 - c) * (1 - 2 * x), slot + c * 2 * (1 - 2 * y)),
             ),
         }
-        z_peers = [((((z + s) % 4) * 2 + x), slot) for s in (1, 2, 3)]
+        z_peers = [((((z + s) % 4) * 2 + x), slot) for s in Z_ORDER]
         diagonal = (z * 2 + 1 - x, (1 - y) * 2 + c)
         peers = [partner, x_peer, y_peer] + z_peers
     else:
@@ -229,7 +230,7 @@
         known = {
             "A": (pa, [(1 - pa, dev_a)]),
             "B": (pb, [(1 - pb, dev_b)]),
-            "Z": (z, [((z + s + 1) % 4, z_peers[s]) for s in range(3)]),
+            "Z": (z, [((z + s) % 4, peer) for s, peer in zip(Z_ORDER, z_peers)]),
             "P": (x * 2 + y, [((1 - x) * 2 + y, x_peer), (x * 2 + 1 - y, y_peer), ((1 - x) * 2 + 1 - y, diagonal)]),
         }
         return [(known[axis][0], step, known[axis][1]) for axis, step in zip(mode[0], strides(mode)[1])]

time: 89.5 us -> 89.5 us (level)
  no operation moved by 1% of the time
where the time goes in v6:
time: 89.5 us; the launch traced here: 89.3 us
  Pallas kernels  88.6 us (99%)
    pallas_call x1, Pallas kernels, run_block(): pl.pallas_call(functools.partial(block_kernel, linked, 12, 2 + len(small)...  84.7 us
    pallas_call x1, Pallas kernels, finish(): pl.pallas_call(finish_kernel, grid=(rows * length // count,), out_shape=[...  3.85 us

profile of v6, /device:TPU:0, one launch (start us, length us, event | category | flops | bytes accessed | tf_op | source)
XLA Modules:
  0.0 89.3 jit_solution(10131858557345134785)
XLA Ops:
  0.6 84.7 %shard_map.203 = (bf16[2,1024,512]{2,1,0:T(8,128)(2,1)S(1)}, bf16[2,1024,512]{2,1,0:T(8,128)(2,1)S(1)}, f32[848,128]{1,0:T(8,128)S(1)}) custom-call(f32[2,1024,512]{2,1,0:T(8,128)} %refs_0_.1, s32[2,1024]{1,0:T(2,128)} %refs_1_.1, f32[2,1024,512]{2,1,0:T(8,128)} %refs_2_.1, bf16[16,512]{1,0:T(8,128)(2,1)} %refs_3_.1, bf16[16,512]{1,0:T(8,128)(2,1)} %refs_4_.1, ...), custom_call_target="tpu_custom_call" | custom-call | tf_op jit(solution)/shard_map/pallas_call | solution.py:934
  85.4 3.9 %shard_map.204 = (f32[2,1024,512]{2,1,0:T(8,128)}, f32[2,1024,512]{2,1,0:T(8,128)}, f32[16,512]{1,0:T(8,128)}, f32[16,512]{1,0:T(8,128)}, f32[16,512]{1,0:T(8,12...) custom-call(bf16[2,1024,512]{2,1,0:T(8,128)(2,1)S(1)} %get-tuple-ele, ...), custom_call_target="tpu_custom_call" | custom-call | tf_op jit(solution)/shard_map/pallas_call | solution.py:874
